TPU v7x, 32 devices: a whole 2x2x4 slice. The times are simulated.
32 devices in a mesh: layer: 16 (over z, x, core), rep: 2 (over y).
Axes of the slice: x: 2, y: 2, z: 4, core: 2. Of those that a mesh axis runs over, the one named last changes fastest.
Arguments:
- gradients: bfloat16 [2, 16, 512, 1024], P('rep', 'layer'), may hold values from -60 to 60
- inverse_out: bfloat16 [16, 512, 512], P('layer', 'rep'), may hold values from -1 to 4
- inverse_in: bfloat16 [16, 1024, 1024], P('layer', 'rep'), may hold values from -1 to 4
- cross_out: bfloat16 [16, 512, 512], P('layer', 'rep'), may hold values from -0.125 to 0.125
- cross_in: bfloat16 [16, 1024, 1024], P('layer', 'rep'), may hold values from -0.1875 to 0.1875
- momentum: float32 [16, 512, 1024], P('layer', 'rep'), may hold values from -3 to 3
Outputs:
- momentum_new: float32 [16, 512, 1024], P('layer', 'rep')
All inputs are finite; a program needn't handle non-finite values.
Results may differ from a plain program's by a relative error of at most 0.003.
Values may be sent and summed in bfloat16 or wider, within the bound.
No kernel may reach another device: no remote copies, remote signals or barrier semaphores. Data moves between devices by JAX's collectives and lax.ppermute only.
A program may use at most 64 MiB of HBM per device.

v0:
```python
import functools

import jax
import jax.numpy as jnp
from jax import lax
from jax.experimental import pallas as pl
from jax.experimental.pallas import tpu as pltpu
from jax.sharding import PartitionSpec as P

SHARES = (2, 1, 1)
EARLY = 2
PARTS = 2
ROWS = 16
TILE = 256
HALF = jnp.bfloat16
FULL = jnp.float32


def passed_along(value, axis, steps):
    count = lax.axis_size(axis)
    initial, last = (max(0, -steps), min(count, count - steps))
    return lax.ppermute(value, axis, [(source, source + steps) for source in range(initial, last)])


def passed_round(value, axis):
    count = lax.axis_size(axis)
    return lax.ppermute(value, axis, [(source, (source + 1) % count) for source in range(count)])


def from_peers(value, axis):
    count = lax.axis_size(axis)
    return [
        lax.ppermute(value, axis, [(source, (source - step) % count) for source in range(count)])
        for step in range(1, count)
    ]


def to_peer(value, axis, step):
    count = lax.axis_size(axis)
    return lax.ppermute(
        value, axis, [(source, (source + step) % count) for source in range(count)]
    )


def dot(left, right, contract=((1,), (0,))):
    return lax.dot_general(left, right, (contract, ((), ())), preferred_element_type=FULL)


def span(me_ref, step, count, size):
    start = lax.rem(me_ref[0] + step, count) * size
    return pl.ds(pl.multiple_of(start, size), size)


def cut_kernel(widths, me, cross_out, inverse_out, inverse_in, pair, *refs):
    pieces, sems = refs[:-1], refs[-1]
    rows, start = cross_out.shape[0], 0
    copies = [
        pltpu.make_async_copy(cross_out, pair.at[:rows], sems.at[0]),
        pltpu.make_async_copy(inverse_out, pair.at[rows:], sems.at[1]),
    ]
    for at, width in enumerate(widths):
        source = inverse_in.at[:, start : start + width]
        copies.append(pltpu.make_async_copy(source, pieces[at], sems.at[2 + at]))
        start += width
    for copy in copies:
        copy.start()
    for copy in copies:
        copy.wait()


def first_kernel(count, me, following, own, *refs):
    others, out = refs[: count - 1], refs[-1]
    rows = own.shape[0]

    @pl.loop(0, out.shape[1] // TILE)
    def _(at):
        columns = pl.ds(pl.multiple_of(at * TILE, TILE), TILE)
        right = following[:, columns]
        out[span(me, 0, count, rows), columns] = dot(own[...], right).astype(HALF)
        for step in range(1, count):
            block = others[step - 1][:rows, :]
            out[span(me, step, count, rows), columns] = dot(block, right).astype(HALF)


def left_kernel(count, me, grads, first, inv_own, *refs):
    rights, others, out = refs[:count], refs[count : 2 * count - 1], refs[2 * count - 1]
    depth, rows = rights[0].shape[0], inv_own.shape[0]

    @pl.loop(0, out.shape[1] // TILE)
    def _(at):
        columns = pl.ds(pl.multiple_of(at * TILE, TILE), TILE)
        cross = sum(
            dot(first[:, span(me, step, count, depth)], rights[step][:, columns])
            for step in range(count)
        )
        residual = (grads[:, columns].astype(FULL) - cross).astype(HALF)
        out[span(me, 0, count, rows), columns] = dot(inv_own[...], residual).astype(HALF)
        for step in range(1, count):
            block = others[step - 1][rows:, :]
            out[span(me, step, count, rows), columns] = dot(block, residual).astype(HALF)


def mine_kernel(count, me, left, inv_own, out):
    @pl.loop(0, out.shape[1] // TILE)
    def _(at):
        columns = pl.ds(pl.multiple_of(at * TILE, TILE), TILE)
        out[:, columns] = dot(left[:, span(me, 0, count, inv_own.shape[0])], inv_own[:, columns])


def chunk_kernel(count, start, me, left, mine, cross_own, *refs):
    pieces, others = refs[: count - 1], refs[count - 1 : 2 * count - 2]
    precond, back = refs[2 * count - 2 :]
    depth, rows = pieces[0].shape[0], cross_own.shape[0]
    product = mine[:, start : start + precond.shape[1]]
    for step in range(1, count):
        product += dot(left[:, span(me, step, count, depth)], pieces[step - 1][...])
    precond[...] = product.astype(HALF)
    turned = ((0,), (0,))
    result = dot(cross_own[...], precond[span(me, 0, count, rows), :], turned)
    for step in range(1, count):
        block = others[step - 1][:rows, :]
        result += dot(block, precond[span(me, step, count, rows), :], turned)
    back[...] = result.astype(HALF)


def stack(target, values, lines=slice(None)):
    start = 0
    for value in values:
        target[:, start : start + value.shape[1]] = value[lines, :]
        start += value.shape[1]


def early_kernel(count, rows, me, *refs):
    total = len(SHARES)
    preconds, backs = refs[:total], refs[total : total + EARLY]
    rights = refs[total + EARLY : total + EARLY + count]
    nears, (staged, stacked) = refs[total + EARLY + count : -2], refs[-2:]
    depth, known, near = rights[0].shape[0], stacked.shape[1], staged.shape[0]
    for row_step in range(1, count):
        start = lax.rem(me[0] + row_step, count) * rows
        lines = pl.ds(pl.multiple_of(start, ROWS), near)
        stack(staged, preconds, lines)
        stack(stacked, backs, lines)
        for step in range(count):
            columns = span(me, step, count, depth)
            product = dot(stacked[...], rights[step][:, :known], ((1,), (1,)))
            update = staged[:, columns].astype(FULL) - product
            nears[row_step - 1][:, columns] = update.astype(HALF)


def gather_kernel(count, me, *refs):
    total = len(SHARES)
    preconds, backs = refs[:total], refs[total : 2 * total - 1]
    rights = refs[2 * total - 1 : 2 * total - 1 + count]
    partial, right_rest, staged, stacked = refs[2 * total - 1 + count :]
    depth, known = rights[0].shape[0], stacked.shape[1]
    stack(staged, preconds)
    stack(stacked, backs)
    for step in range(count):
        columns = span(me, step, count, depth)
        right_rest[columns, :] = rights[step][:, right_rest.shape[0] - right_rest.shape[1] :]
        right = rights[step][:, :known]
        for row in range(0, staged.shape[0], TILE):
            here = slice(row, row + TILE)
            product = dot(stacked[here, :], right, ((1,), (1,)))
            partial[here, columns] = staged[here, columns].astype(FULL) - product


def update_kernel(count, me, partial, right_rest, *refs):
    late = len(SHARES) - EARLY
    backs, (squares, own), refs = refs[:late], refs[late : late + 2], refs[late + 2 :]
    rests, fars = refs[: count - 1], refs[count - 1 :]
    rows, wide = own.shape
    back, total = backs[-1], jnp.zeros((), FULL)
    skipped = right_rest.shape[1] - back.shape[1]
    for step in range(count):
        here = span(me, step, count, rows)
        for start in range(0, wide, TILE):
            columns = slice(start, start + TILE)
            update = partial[here, columns] - dot(
                back[here, :], right_rest[columns, skipped:], ((1,), (1,))
            )
            total += jnp.sum(update * update)
            if step == 0:
                own[:, columns] = update
            else:
                row = rests[step - 1].shape[0]
                for far in fars[(step - 1) * PARTS : step * PARTS]:
                    far[:, columns] = update[row : row + far.shape[0]].astype(HALF)
                    row += far.shape[0]
        if step:
            start = lax.rem(me[0] + step, count) * rows
            lines = pl.ds(pl.multiple_of(start, ROWS), rests[step - 1].shape[0])
            stack(rests[step - 1], backs, lines)
    squares[...] = jnp.full(squares.shape, total, FULL)


def scale_of(squares, size):
    return lax.rsqrt(squares * (1.0 / size) + 1e-06)


def base_kernel(count, size, momentum, squares, own, out):
    scale = scale_of(squares[0:1, 0:1], size) * (1.0 / count)
    out[...] = 0.9 * momentum[...] + own[...] * scale


def final_kernel(count, size, base, right_rest, *refs):
    peers = count - 1
    others, nears, rests = (refs[at * peers : (at + 1) * peers] for at in range(3))
    fars = refs[3 * peers : (3 + PARTS) * peers]
    out, scratch, sems = refs[-3:]
    scales = [scale_of(value[0:1, 0:1], size) * (1.0 / count) for value in others]
    copies, row = [], nears[0].shape[0]
    for at in range(PARTS + 1):
        if at < PARTS:
            here = slice(row, row + fars[at].shape[0])
            row = here.stop
        else:
            here = slice(0, nears[0].shape[0])
        total = base[here, :]
        for step in range(peers):
            if at < PARTS:
                update = fars[step * PARTS + at][...].astype(FULL)
            else:
                rest = dot(rests[step][...], right_rest[...], ((1,), (1,)))
                update = nears[step][...].astype(FULL) - rest
            total += update * scales[step]
        scratch[here, :] = total
        copies.append(pltpu.make_async_copy(scratch.at[here, :], out.at[here, :], sems.at[at]))
        copies[-1].start()
    for copy in copies:
        copy.wait()


def call(kernel, outs, operands, flops, **options):
    moved = sum(value.size * value.dtype.itemsize for value in (*operands, *outs))
    vmem = pl.BlockSpec(memory_space=pltpu.VMEM)
    specs = [pl.BlockSpec(memory_space=pltpu.SMEM)] + [vmem] * (len(operands) - 1)
    settings = dict(in_specs=specs, out_specs=[vmem] * len(outs))
    settings.update(options)
    return pl.pallas_call(
        kernel,
        out_shape=outs,
        compiler_params=pltpu.CompilerParams(vmem_limit_bytes=16 * 1024 * 1024),
        cost_estimate=pl.CostEstimate(flops=flops, bytes_accessed=moved // 64, transcendentals=0),
        **settings,
    )(*operands)


def body(gradients, inverse_out, inverse_in, cross_out, cross_in, momentum):
    own_block = gradients[0, 0]
    tall, wide = own_block.shape
    count = lax.axis_size("rep")
    me = lax.axis_index("rep").astype(jnp.int32).reshape(1)
    widths = [share * wide // sum(SHARES) for share in SHARES]
    rows = momentum.shape[1]
    shape = jax.ShapeDtypeStruct
    part = functools.partial

    anywhere = pl.BlockSpec(memory_space=pl.ANY)
    out_rows, out_wide = cross_out.shape[1:]
    pair, *cuts = call(
        part(cut_kernel, widths),
        [shape((2 * out_rows, out_wide), HALF)]
        + [shape((inverse_in.shape[1], width), HALF) for width in widths],
        [me, cross_out[0], inverse_out[0], inverse_in[0]],
        0,
        in_specs=[pl.BlockSpec(memory_space=pltpu.SMEM)] + [anywhere] * 3,
        scratch_shapes=[pltpu.SemaphoreType.DMA((2 + len(widths),))],
    )
    pairs = from_peers(pair, "rep")
    in_blocks = [cross_in[0], *from_peers(cross_in[0], "rep")]
    following = passed_along(own_block, "layer", -1)

    cut_peers = [from_peers(piece, "rep") for piece in cuts]
    (first,) = call(
        part(first_kernel, count),
        [shape((tall, wide), HALF)],
        [me, following, cross_out[0], *pairs],
        tall * tall * wide // 32,
    )
    previous_blocks = [passed_along(block, "layer", 1) for block in in_blocks]
    (left,) = call(
        part(left_kernel, count),
        [shape((tall, wide), HALF)],
        [me, own_block, first, inverse_out[0], *in_blocks, *pairs],
        tall * wide * (tall + wide) // 32,
    )
    (mine,) = call(
        part(mine_kernel, count),
        [shape((tall, wide), FULL)],
        [me, left, inverse_in[0]],
        tall * wide * wide // 64,
    )
    preconds, backs = [], []
    for at, peers in enumerate(cut_peers):
        precond, back = call(
            part(chunk_kernel, count, sum(widths[:at])),
            [shape((tall, widths[at]), HALF)] * 2,
            [me, left, mine, cross_out[0], *peers, *pairs],
            tall * widths[at] * (tall + wide) // 32,
        )
        preconds.append(precond)
        ring = at != 1
        backs.append(passed_round(back, "layer") if ring else passed_along(back, "layer", 1))
    near = 3 * rows // 8 // ROWS * ROWS
    peers, last, later = count - 1, widths[-1], sum(widths[EARLY:])
    far_rows, left_rows = [], rows - near
    for at in range(PARTS, 0, -1):
        far_rows.append(left_rows if at == 1 else left_rows // at // ROWS * ROWS)
        left_rows -= far_rows[-1]
    nears = call(
        part(early_kernel, count, rows),
        [shape((near, wide), HALF)] * peers,
        [me, *preconds, *backs[:EARLY], *previous_blocks],
        2 * peers * near * wide * (wide - later),
        scratch_shapes=[pltpu.VMEM((near, wide), HALF), pltpu.VMEM((near, wide - later), HALF)],
    )
    nears = [to_peer(value, "rep", at + 1) for at, value in enumerate(nears)]
    partial, right_rest = call(
        part(gather_kernel, count),
        [shape((tall, wide), FULL), shape((wide, later), HALF)],
        [me, *preconds, *backs[:-1], *previous_blocks],
        2 * tall * wide * (wide - last),
        scratch_shapes=[pltpu.VMEM((tall, wide), HALF), pltpu.VMEM((tall, wide - last), HALF)],
    )
    squares, own, *sends = call(
        part(update_kernel, count),
        [shape((8, 128), FULL), shape((rows, wide), FULL)]
        + [shape((near, later), HALF)] * peers
        + [shape((size, wide), HALF) for size in far_rows] * peers,
        [me, partial, right_rest, *backs[EARLY:]],
        2 * tall * wide * last,
    )
    rests = [to_peer(value, "rep", at + 1) for at, value in enumerate(sends[:peers])]
    fars = [to_peer(value, "rep", at // PARTS + 1) for at, value in enumerate(sends[peers:])]
    others = [to_peer(squares, "rep", step) for step in range(1, count)]
    (base,) = call(
        part(base_kernel, count, tall * wide),
        [shape((rows, wide), FULL)],
        [momentum[0], squares, own],
        2 * rows * wide,
        in_specs=[pl.BlockSpec(memory_space=pltpu.VMEM)] * 3,
    )
    operands = [base, right_rest, *others, *nears, *rests, *fars]
    (result,) = call(
        part(final_kernel, count, tall * wide),
        [shape((rows, wide), FULL)],
        operands,
        4 * rows * wide,
        in_specs=[pl.BlockSpec(memory_space=pltpu.VMEM)] * len(operands),
        out_specs=[anywhere],
        scratch_shapes=[pltpu.VMEM((rows, wide), FULL), pltpu.SemaphoreType.DMA((PARTS + 1,))],
    )
    return result[None]


def solution(mesh):
    in_specs = (
        P("rep", "layer", None, None),
        P("layer", "rep", None),
        P("layer", "rep", None),
        P("layer", "rep", None),
        P("layer", "rep", None),
        P("layer", "rep", None),
    )
    out_specs = P("layer", "rep", None)
    return jax.shard_map(body, mesh=mesh, in_specs=in_specs, out_specs=out_specs, check_vma=False)
```

profile of v0, /device:TPU:0, one launch (start us, length us, event | category | flops | bytes accessed | tf_op | source)
XLA Modules:
  0.0 79.2 jit_solution(14524671236700877463)
XLA Ops:
  0.0 3.0 %collective-permute-start.2 = (bf16[512,1024]{1,0:T(8,128)(2,1)}, bf16[512,1024]{1,0:T(8,128)(2,1)S(1)}, u32[]{:S(2)}, u32[]{:S(2)}) collective-permute-start(bf16[512,1024]{1,0:T(8,128)(2,1)} %bitcast.20), channel_id=1, source_target_pairs={{0,1},{1,0},{2,3},{3,2},{4,5},{5,4},{6,7},{7,6},{8,9},{9,8},{10,11... | collective-permute-start | bytes 3145736 | tf_op jit(solution)/shard_map/ppermute | solution.py:33
  3.0 1.3 %collective-permute-start = (bf16[512,1024]{1,0:T(8,128)(2,1)}, bf16[512,1024]{1,0:T(8,128)(2,1)S(1)}, u32[]{:S(2)}, u32[]{:S(2)}) collective-permute-start(bf16[512,1024]{1,0:T(8,128)(2,1)} %bitcast.18), channel_id=1, source_target_pairs={{2,0},{4,2},{6,4},{8,6},{10,8},{12,10},{14,12},{16,14},{18,16},{20... | collective-permute-start | bytes 3145736 | tf_op jit(solution)/shard_map/ppermute | solution.py:22
  4.3 0.9 %copy-done = bf16[1,256,512]{2,1,0:T(8,128)(2,1)S(1)} copy-done((bf16[1,256,512]{2,1,0:T(8,128)(2,1)S(1)}, bf16[1,256,512]{2,1,0:T(8,128)(2,1)}, u32[]{:S(2)}) %copy-start) | copy-done | bytes 262168
  5.2 1.2 %copy-done.2 = bf16[1,512,1024]{2,1,0:T(8,128)(2,1)S(1)} copy-done((bf16[1,512,1024]{2,1,0:T(8,128)(2,1)S(1)}, bf16[1,512,1024]{2,1,0:T(8,128)(2,1)}, u32[]{:S(2)}) %copy-start.2) | copy-done | bytes 1048600
  6.4 0.9 %copy-done.5 = bf16[1,256,512]{2,1,0:T(8,128)(2,1)S(1)} copy-done((bf16[1,256,512]{2,1,0:T(8,128)(2,1)S(1)}, bf16[1,256,512]{2,1,0:T(8,128)(2,1)}, u32[]{:S(2)}) %copy-start.5) | copy-done | bytes 262168
  7.7 2.0 %collective-permute-start.3 = (bf16[512,512]{1,0:T(8,128)(2,1)S(1)}, bf16[512,512]{1,0:T(8,128)(2,1)S(1)}, u32[]{:S(2)}, u32[]{:S(2)}) collective-permute-start(bf16[512,512]{1,0:T(8,128)(2,1)S(1)} %get-tuple-element.23), channel_id=1, source_target_pairs={{0,1},{1,0},{2,3},{3,2},{4,5},{5,4},{6,7},{7,6},{8,9},{9,8},{10,11... | collective-permute-start | bytes 1572872 | tf_op jit(solution)/shard_map/ppermute | solution.py:33
  9.7 2.5 %collective-permute-start.8 = (bf16[512,1024]{1,0:T(8,128)(2,1)}, bf16[512,1024]{1,0:T(8,128)(2,1)S(1)}, u32[]{:S(2)}, u32[]{:S(2)}) collective-permute-start(bf16[512,1024]{1,0:T(8,128)(2,1)} %bitcast.21), channel_id=1, source_target_pairs={{0,2},{2,4},{4,6},{6,8},{8,10},{10,12},{12,14},{14,16},{16,18},{18... | collective-permute-start | bytes 3145736 | tf_op jit(solution)/shard_map/ppermute | solution.py:22
  12.3 14.9 %collective-permute-done.2.refs_1_ = bf16[512,1024]{1,0:T(8,128)(2,1)S(1)} collective-permute-done((bf16[512,1024]{1,0:T(8,128)(2,1)}, bf16[512,1024]{1,0:T(8,128)(2,1)S(1)}, u32[]{:S(2)}, u32[]{:S(2)}) %collective-permute-start.2) | collective-permute-done | bytes 1048608 | tf_op jit(solution)/shard_map/ppermute | solution.py:33
  27.2 1.3 %collective-permute-start.9 = (bf16[512,1024]{1,0:T(8,128)(2,1)S(1)}, bf16[512,1024]{1,0:T(8,128)(2,1)S(1)}, u32[]{:S(2)}, u32[]{:S(2)}) collective-permute-start(bf16[512,1024]{1,0:T(8,128)(2,1)S(1)} %collective-permute-done.2.refs_1_), channel_id=1, source_target_pairs={{0,2},{2,4},{4,6},{6,8},{8,10},{10,12},{12,14},{14,16},{16,18},{18... | collective-permute-start | bytes 3145736 | tf_op jit(solution)/shard_map/ppermute | solution.py:22
  28.5 9.9 %collective-permute-done.1.refs_0_.refs_2_.refs_1_ = bf16[512,512]{1,0:T(8,128)(2,1)S(1)} collective-permute-done((bf16[512,512]{1,0:T(8,128)(2,1)S(1)}, bf16[512,512]{1,0:T(8,128)(2,1)S(1)}, u32[]{:S(2)}, u32[]{:S(2)}) %collective-permute-start.1) | collective-permute-done | bytes 524320 | tf_op jit(solution)/shard_map/ppermute | solution.py:33
  38.4 2.1 %collective-permute-start.4 = (bf16[512,256]{1,0:T(8,128)(2,1)S(1)}, bf16[512,256]{1,0:T(8,128)(2,1)S(1)}, u32[]{:S(2)}, u32[]{:S(2)}) collective-permute-start(bf16[512,256]{1,0:T(8,128)(2,1)S(1)} %get-tuple-element.25), channel_id=1, source_target_pairs={{0,1},{1,0},{2,3},{3,2},{4,5},{5,4},{6,7},{7,6},{8,9},{9,8},{10,11... | collective-permute-start | bytes 786440 | tf_op jit(solution)/shard_map/ppermute | solution.py:33
  40.5 1.3 %shard_map.65.first = bf16[512,1024]{1,0:T(8,128)(2,1)S(1)} custom-call(s32[1]{0:T(128)} %bitcast.1.me, bf16[512,1024]{1,0:T(8,128)(2,1)S(1)} %collective-permute-done.following, bf16[256,512]{1,0:T(8,128)(2,1)S(1)} %bitcast.9, bf16[512,512]{1,0:T(8,128)(2,1)S(1)} %collective-permute-done.1.refs_0_.refs_2_.refs_1_), custom_call_target="tpu_custom_call" | custom-call | flops 8388608 | bytes 45056 | tf_op jit(solution)/shard_map/pallas_call | solution.py:241
  41.8 3.6 %shard_map.66.left = bf16[512,1024]{1,0:T(8,128)(2,1)S(1)} custom-call(s32[1]{0:T(128)} %bitcast.1.me, bf16[512,1024]{1,0:T(8,128)(2,1)S(1)} %bitcast.19, bf16[512,1024]{1,0:T(8,128)(2,1)S(1)} %shard_map.65.first, bf16[256,512]{1,0:T(8,128)(2,1)S(1)} %bitcast.17, bf16[512,1024]{1,0:T(8,128)(2,1)S(1)} %bitcast.22, ...), custom_call_target="tpu_custom_call" | custom-call | flops 25165824 | bytes 94208 | tf_op jit(solution)/shard_map/pallas_call | solution.py:241
  45.4 1.2 %shard_map.67.mine = f32[512,1024]{1,0:T(8,128)S(1)} custom-call(s32[1]{0:T(128)} %bitcast.1.me, bf16[512,1024]{1,0:T(8,128)(2,1)S(1)} %shard_map.66.left, bf16[512,1024]{1,0:T(8,128)(2,1)S(1)} %bitcast.14), custom_call_target="tpu_custom_call" | custom-call | flops 8388608 | bytes 65536 | tf_op jit(solution)/shard_map/pallas_call | solution.py:241
  46.6 3.0 %collective-permute-done.3.refs_0_ = bf16[512,512]{1,0:T(8,128)(2,1)S(1)} collective-permute-done((bf16[512,512]{1,0:T(8,128)(2,1)S(1)}, bf16[512,512]{1,0:T(8,128)(2,1)S(1)}, u32[]{:S(2)}, u32[]{:S(2)}) %collective-permute-start.3) | collective-permute-done | bytes 524320 | tf_op jit(solution)/shard_map/ppermute | solution.py:33
  49.6 0.9 %shard_map.68 = (bf16[512,512]{1,0:T(8,128)(2,1)S(1)}, bf16[512,512]{1,0:T(8,128)(2,1)S(1)}) custom-call(s32[1]{0:T(128)} %bitcast.1.me, bf16[512,1024]{1,0:T(8,128)(2,1)S(1)} %shard_map.66.left, f32[512,1024]{1,0:T(8,128)S(1)} %shard_map.67.mine, bf16[256,512]{1,0:T(8,128)(2,1)S(1)} %bitcast.10, bf16[512,512]{1,0:T(8,128)(2,1)S(1)} %collective-permute-done.3.refs_0_, ...), custom_call_target="tpu_custom_call" | custom-call | flops 12582912 | bytes 86016 | tf_op jit(solution)/shard_map/pallas_call | solution.py:241
  50.6 2.1 %collective-permute-start.5 = (bf16[512,256]{1,0:T(8,128)(2,1)S(1)}, bf16[512,256]{1,0:T(8,128)(2,1)S(1)}, u32[]{:S(2)}, u32[]{:S(2)}) collective-permute-start(bf16[512,256]{1,0:T(8,128)(2,1)S(1)} %get-tuple-element.27), channel_id=1, source_target_pairs={{0,1},{1,0},{2,3},{3,2},{4,5},{5,4},{6,7},{7,6},{8,9},{9,8},{10,11... | collective-permute-start | bytes 786440 | tf_op jit(solution)/shard_map/ppermute | solution.py:33
  52.7 1.7 %collective-permute-done.4.refs_0_ = bf16[512,256]{1,0:T(8,128)(2,1)S(1)} collective-permute-done((bf16[512,256]{1,0:T(8,128)(2,1)S(1)}, bf16[512,256]{1,0:T(8,128)(2,1)S(1)}, u32[]{:S(2)}, u32[]{:S(2)}) %collective-permute-start.4) | collective-permute-done | bytes 262176 | tf_op jit(solution)/shard_map/ppermute | solution.py:33
  54.4 0.8 %shard_map.69 = (bf16[512,256]{1,0:T(8,128)(2,1)S(1)}, bf16[512,256]{1,0:T(8,128)(2,1)S(1)}) custom-call(s32[1]{0:T(128)} %bitcast.1.me, bf16[512,1024]{1,0:T(8,128)(2,1)S(1)} %shard_map.66.left, f32[512,1024]{1,0:T(8,128)S(1)} %shard_map.67.mine, bf16[256,512]{1,0:T(8,128)(2,1)S(1)} %bitcast.11, bf16[512,256]{1,0:T(8,128)(2,1)S(1)} %collective-permute-done.4.refs_0_, ...), custom_call_target="tpu_custom_call" | custom-call | flops 6291456 | bytes 73728 | tf_op jit(solution)/shard_map/pallas_call | solution.py:241
  55.3 1.5 %collective-permute-start.7 = (bf16[512,256]{1,0:T(8,128)(2,1)S(1)}, bf16[512,256]{1,0:T(8,128)(2,1)S(1)}, u32[]{:S(2)}, u32[]{:S(2)}) collective-permute-start(bf16[512,256]{1,0:T(8,128)(2,1)S(1)} %get-tuple-element.30), channel_id=1, source_target_pairs={{0,2},{2,4},{4,6},{6,8},{8,10},{10,12},{12,14},{14,16},{16,18},{18... | collective-permute-start | bytes 786440 | tf_op jit(solution)/shard_map/ppermute | solution.py:22
  56.8 2.3 %collective-permute-done.5.refs_0_ = bf16[512,256]{1,0:T(8,128)(2,1)S(1)} collective-permute-done((bf16[512,256]{1,0:T(8,128)(2,1)S(1)}, bf16[512,256]{1,0:T(8,128)(2,1)S(1)}, u32[]{:S(2)}, u32[]{:S(2)}) %collective-permute-start.5) | collective-permute-done | bytes 262176 | tf_op jit(solution)/shard_map/ppermute | solution.py:33
  59.1 0.8 %shard_map.70 = (bf16[512,256]{1,0:T(8,128)(2,1)S(1)}, bf16[512,256]{1,0:T(8,128)(2,1)S(1)}) custom-call(s32[1]{0:T(128)} %bitcast.1.me, bf16[512,1024]{1,0:T(8,128)(2,1)S(1)} %shard_map.66.left, f32[512,1024]{1,0:T(8,128)S(1)} %shard_map.67.mine, bf16[256,512]{1,0:T(8,128)(2,1)S(1)} %bitcast.12, bf16[512,256]{1,0:T(8,128)(2,1)S(1)} %collective-permute-done.5.refs_0_, ...), custom_call_target="tpu_custom_call" | custom-call | flops 6291456 | bytes 73728 | tf_op jit(solution)/shard_map/pallas_call | solution.py:241
  59.9 1.2 %collective-permute-start.10 = (bf16[512,256]{1,0:T(8,128)(2,1)S(1)}, bf16[512,256]{1,0:T(8,128)(2,1)S(1)}, u32[]{:S(2)}, u32[]{:S(2)}) collective-permute-start(bf16[512,256]{1,0:T(8,128)(2,1)S(1)} %get-tuple-element.33), channel_id=1, source_target_pairs={{0,2},{2,4},{4,6},{6,8},{8,10},{10,12},{12,14},{14,16},{16,18},{18... | collective-permute-start | bytes 786440 | tf_op jit(solution)/shard_map/ppermute | solution.py:27
  61.1 0.8 %collective-permute-done.6.refs_3_ = bf16[512,512]{1,0:T(8,128)(2,1)S(1)} collective-permute-done((bf16[512,512]{1,0:T(8,128)(2,1)S(1)}, bf16[512,512]{1,0:T(8,128)(2,1)S(1)}, u32[]{:S(2)}, u32[]{:S(2)}) %collective-permute-start.6) | collective-permute-done | bytes 524320 | tf_op jit(solution)/shard_map/ppermute | solution.py:27
  61.9 0.6 shard_map.74
  62.5 2.1 %collective-permute-start.12 = (bf16[96,1024]{1,0:T(8,128)(2,1)S(1)}, bf16[96,1024]{1,0:T(8,128)(2,1)S(1)}, u32[]{:S(2)}, u32[]{:S(2)}) collective-permute-start(bf16[96,1024]{1,0:T(8,128)(2,1)S(1)} %shard_map.74), channel_id=1, source_target_pairs={{0,1},{1,0},{2,3},{3,2},{4,5},{5,4},{6,7},{7,6},{8,9},{9,8},{10,11... | collective-permute-start | bytes 589832 | tf_op jit(solution)/shard_map/ppermute | solution.py:40
  64.6 1.1 %shard_map.71 = (f32[512,1024]{1,0:T(8,128)S(1)}, bf16[1024,256]{1,0:T(8,128)(2,1)S(1)}) custom-call(s32[1]{0:T(128)} %bitcast.1.me, bf16[512,512]{1,0:T(8,128)(2,1)S(1)} %get-tuple-element.24.refs_0_, bf16[512,256]{1,0:T(8,128)(2,1)S(1)} %get-tuple-element.26.refs_1_, bf16[512,256]{1,0:T(8,128)(2,1)S(1)} %get-tuple-element.28.refs_2_, ...), custom_call_target="tpu_custom_call" | custom-call | flops 805306368 | bytes 102400 | tf_op jit(solution)/shard_map/pallas_call | solution.py:241
  65.7 3.0 %collective-permute-done.10.refs_0_ = bf16[512,256]{1,0:T(8,128)(2,1)S(1)} collective-permute-done((bf16[512,256]{1,0:T(8,128)(2,1)S(1)}, bf16[512,256]{1,0:T(8,128)(2,1)S(1)}, u32[]{:S(2)}, u32[]{:S(2)}) %collective-permute-start.10) | collective-permute-done | bytes 262176 | tf_op jit(solution)/shard_map/ppermute | solution.py:27
  69.3 2.2 %collective-permute-start.14 = (bf16[80,1024]{1,0:T(8,128)(2,1)S(1)}, bf16[80,1024]{1,0:T(8,128)(2,1)S(1)}, u32[]{:S(2)}, u32[]{:S(2)}) collective-permute-start(bf16[80,1024]{1,0:T(8,128)(2,1)S(1)} %get-tuple-element.37), channel_id=1, source_target_pairs={{0,1},{1,0},{2,3},{3,2},{4,5},{5,4},{6,7},{7,6},{8,9},{9,8},{10,11... | collective-permute-start | bytes 491528 | tf_op jit(solution)/shard_map/ppermute | solution.py:40
  71.5 1.9 %collective-permute-start.13 = (bf16[96,256]{1,0:T(8,128)(2,1)S(1)}, bf16[96,256]{1,0:T(8,128)(2,1)S(1)}, u32[]{:S(2)}, u32[]{:S(2)}) collective-permute-start(bf16[96,256]{1,0:T(8,128)(2,1)S(1)} %get-tuple-element.36), channel_id=1, source_target_pairs={{0,1},{1,0},{2,3},{3,2},{4,5},{5,4},{6,7},{7,6},{8,9},{9,8},{10,11... | collective-permute-start | bytes 147464 | tf_op jit(solution)/shard_map/ppermute | solution.py:40
  73.8 4.2 %collective-permute-done.11.refs_0_ = f32[8,128]{1,0:T(8,128)S(1)} collective-permute-done((f32[8,128]{1,0:T(8,128)S(1)}, f32[8,128]{1,0:T(8,128)S(1)}, u32[]{:S(2)}, u32[]{:S(2)}) %collective-permute-start.11) | collective-permute-done | bytes 4128 | tf_op jit(solution)/shard_map/ppermute | solution.py:40
  78.1 1.2 %shard_map.75 = f32[256,1024]{1,0:T(8,128)} custom-call(f32[256,1024]{1,0:T(8,128)S(1)} %shard_map.73.base, bf16[1024,256]{1,0:T(8,128)(2,1)S(1)} %get-tuple-element.32.right_rest, f32[8,128]{1,0:T(8,128)S(1)} %collective-permute-done.11.refs_0_, bf16[96,1024]{1,0:T(8,128)(2,1)S(1)} %collective-permute-done.12.refs_1_, ...), custom_call_target="tpu_custom_call" | custom-call | flops 1048576 | bytes 49984 | tf_op jit(solution)/shard_map/pallas_call | solution.py:241
  (28 shorter events, 1.4 us)
Async XLA Ops:
  0.0 27.2 %collective-permute-start.2 = (bf16[512,1024]{1,0:T(8,128)(2,1)}, bf16[512,1024]{1,0:T(8,128)(2,1)S(1)}, u32[]{:S(2)}, u32[]{:S(2)}) collective-permute-start(bf16[512,1024]{1,0:T(8,128)(2,1)} %bitcast.20), channel_id=1, source_target_pairs={{0,1},{1,0},{2,3},{3,2},{4,5},{5,4},{6,7},{7,6},{8,9},{9,8},{10,11... | collective-permute-start | bytes 3145736 | tf_op jit(solution)/shard_map/ppermute | solution.py:33
  3.0 37.5 %collective-permute-start = (bf16[512,1024]{1,0:T(8,128)(2,1)}, bf16[512,1024]{1,0:T(8,128)(2,1)S(1)}, u32[]{:S(2)}, u32[]{:S(2)}) collective-permute-start(bf16[512,1024]{1,0:T(8,128)(2,1)} %bitcast.18), channel_id=1, source_target_pairs={{2,0},{4,2},{6,4},{8,6},{10,8},{12,10},{14,12},{16,14},{18,16},{20... | collective-permute-start | bytes 3145736 | tf_op jit(solution)/shard_map/ppermute | solution.py:22
  4.3 1.0 %copy-start = (bf16[1,256,512]{2,1,0:T(8,128)(2,1)S(1)}, bf16[1,256,512]{2,1,0:T(8,128)(2,1)}, u32[]{:S(2)}) copy-start(bf16[1,256,512]{2,1,0:T(8,128)(2,1)} %param.9) | copy-start | bytes 786436
  5.2 1.2 %copy-start.2 = (bf16[1,512,1024]{2,1,0:T(8,128)(2,1)S(1)}, bf16[1,512,1024]{2,1,0:T(8,128)(2,1)}, u32[]{:S(2)}) copy-start(bf16[1,512,1024]{2,1,0:T(8,128)(2,1)} %param.8) | copy-start | bytes 3145732
  6.4 0.9 %copy-start.5 = (bf16[1,256,512]{2,1,0:T(8,128)(2,1)S(1)}, bf16[1,256,512]{2,1,0:T(8,128)(2,1)}, u32[]{:S(2)}) copy-start(bf16[1,256,512]{2,1,0:T(8,128)(2,1)} %param.7) | copy-start | bytes 786436
  7.4 34.4 %copy-start.6 = (bf16[1,1,512,1024]{3,2,1,0:T(8,128)(2,1)S(1)}, bf16[1,1,512,1024]{3,2,1,0:T(8,128)(2,1)}, u32[]{:S(2)}) copy-start(bf16[1,1,512,1024]{3,2,1,0:T(8,128)(2,1)} %param.6) | copy-start | bytes 3145732
  7.4 34.4 %copy-start.7 = (bf16[1,512,1024]{2,1,0:T(8,128)(2,1)S(1)}, bf16[1,512,1024]{2,1,0:T(8,128)(2,1)}, u32[]{:S(2)}) copy-start(bf16[1,512,1024]{2,1,0:T(8,128)(2,1)} %param.10) | copy-start | bytes 3145732
  7.6 30.8 %collective-permute-start.1 = (bf16[512,512]{1,0:T(8,128)(2,1)S(1)}, bf16[512,512]{1,0:T(8,128)(2,1)S(1)}, u32[]{:S(2)}, u32[]{:S(2)}) collective-permute-start(bf16[512,512]{1,0:T(8,128)(2,1)S(1)} %get-tuple-element.22), channel_id=1, source_target_pairs={{0,1},{1,0},{2,3},{3,2},{4,5},{5,4},{6,7},{7,6},{8,9},{9,8},{10,11... | collective-permute-start | bytes 1572872 | tf_op jit(solution)/shard_map/ppermute | solution.py:33
  7.7 41.9 %collective-permute-start.3 = (bf16[512,512]{1,0:T(8,128)(2,1)S(1)}, bf16[512,512]{1,0:T(8,128)(2,1)S(1)}, u32[]{:S(2)}, u32[]{:S(2)}) collective-permute-start(bf16[512,512]{1,0:T(8,128)(2,1)S(1)} %get-tuple-element.23), channel_id=1, source_target_pairs={{0,1},{1,0},{2,3},{3,2},{4,5},{5,4},{6,7},{7,6},{8,9},{9,8},{10,11... | collective-permute-start | bytes 1572872 | tf_op jit(solution)/shard_map/ppermute | solution.py:33
  9.7 51.3 %collective-permute-start.8 = (bf16[512,1024]{1,0:T(8,128)(2,1)}, bf16[512,1024]{1,0:T(8,128)(2,1)S(1)}, u32[]{:S(2)}, u32[]{:S(2)}) collective-permute-start(bf16[512,1024]{1,0:T(8,128)(2,1)} %bitcast.21), channel_id=1, source_target_pairs={{0,2},{2,4},{4,6},{6,8},{8,10},{10,12},{12,14},{14,16},{16,18},{18... | collective-permute-start | bytes 3145736 | tf_op jit(solution)/shard_map/ppermute | solution.py:22
  27.2 34.7 %collective-permute-start.9 = (bf16[512,1024]{1,0:T(8,128)(2,1)S(1)}, bf16[512,1024]{1,0:T(8,128)(2,1)S(1)}, u32[]{:S(2)}, u32[]{:S(2)}) collective-permute-start(bf16[512,1024]{1,0:T(8,128)(2,1)S(1)} %collective-permute-done.2.refs_1_), channel_id=1, source_target_pairs={{0,2},{2,4},{4,6},{6,8},{8,10},{10,12},{12,14},{14,16},{16,18},{18... | collective-permute-start | bytes 3145736 | tf_op jit(solution)/shard_map/ppermute | solution.py:22
  38.4 16.0 %collective-permute-start.4 = (bf16[512,256]{1,0:T(8,128)(2,1)S(1)}, bf16[512,256]{1,0:T(8,128)(2,1)S(1)}, u32[]{:S(2)}, u32[]{:S(2)}) collective-permute-start(bf16[512,256]{1,0:T(8,128)(2,1)S(1)} %get-tuple-element.25), channel_id=1, source_target_pairs={{0,1},{1,0},{2,3},{3,2},{4,5},{5,4},{6,7},{7,6},{8,9},{9,8},{10,11... | collective-permute-start | bytes 786440 | tf_op jit(solution)/shard_map/ppermute | solution.py:33
  41.8 3.6 %copy-start.3 = (bf16[1,512,1024]{2,1,0:T(8,128)(2,1)S(1)}, bf16[1,512,1024]{2,1,0:T(8,128)(2,1)}, u32[]{:S(2)}) copy-start(bf16[1,512,1024]{2,1,0:T(8,128)(2,1)} %param.8) | copy-start | bytes 3145732
  45.4 4.3 %copy-start.1 = (bf16[1,256,512]{2,1,0:T(8,128)(2,1)S(1)}, bf16[1,256,512]{2,1,0:T(8,128)(2,1)}, u32[]{:S(2)}) copy-start(bf16[1,256,512]{2,1,0:T(8,128)(2,1)} %param.9) | copy-start | bytes 786436
  50.5 11.4 %collective-permute-start.6 = (bf16[512,512]{1,0:T(8,128)(2,1)S(1)}, bf16[512,512]{1,0:T(8,128)(2,1)S(1)}, u32[]{:S(2)}, u32[]{:S(2)}) collective-permute-start(bf16[512,512]{1,0:T(8,128)(2,1)S(1)} %get-tuple-element.29), channel_id=1, source_target_pairs={{0,2},{2,4},{4,6},{6,8},{8,10},{10,12},{12,14},{14,16},{16,18},{18... | collective-permute-start | bytes 1572872 | tf_op jit(solution)/shard_map/ppermute | solution.py:27
  50.6 8.4 %collective-permute-start.5 = (bf16[512,256]{1,0:T(8,128)(2,1)S(1)}, bf16[512,256]{1,0:T(8,128)(2,1)S(1)}, u32[]{:S(2)}, u32[]{:S(2)}) collective-permute-start(bf16[512,256]{1,0:T(8,128)(2,1)S(1)} %get-tuple-element.27), channel_id=1, source_target_pairs={{0,1},{1,0},{2,3},{3,2},{4,5},{5,4},{6,7},{7,6},{8,9},{9,8},{10,11... | collective-permute-start | bytes 786440 | tf_op jit(solution)/shard_map/ppermute | solution.py:33
  55.3 5.8 %collective-permute-start.7 = (bf16[512,256]{1,0:T(8,128)(2,1)S(1)}, bf16[512,256]{1,0:T(8,128)(2,1)S(1)}, u32[]{:S(2)}, u32[]{:S(2)}) collective-permute-start(bf16[512,256]{1,0:T(8,128)(2,1)S(1)} %get-tuple-element.30), channel_id=1, source_target_pairs={{0,2},{2,4},{4,6},{6,8},{8,10},{10,12},{12,14},{14,16},{16,18},{18... | collective-permute-start | bytes 786440 | tf_op jit(solution)/shard_map/ppermute | solution.py:22
  59.9 8.8 %collective-permute-start.10 = (bf16[512,256]{1,0:T(8,128)(2,1)S(1)}, bf16[512,256]{1,0:T(8,128)(2,1)S(1)}, u32[]{:S(2)}, u32[]{:S(2)}) collective-permute-start(bf16[512,256]{1,0:T(8,128)(2,1)S(1)} %get-tuple-element.33), channel_id=1, source_target_pairs={{0,2},{2,4},{4,6},{6,8},{8,10},{10,12},{12,14},{14,16},{16,18},{18... | collective-permute-start | bytes 786440 | tf_op jit(solution)/shard_map/ppermute | solution.py:27
  62.5 15.5 %collective-permute-start.12 = (bf16[96,1024]{1,0:T(8,128)(2,1)S(1)}, bf16[96,1024]{1,0:T(8,128)(2,1)S(1)}, u32[]{:S(2)}, u32[]{:S(2)}) collective-permute-start(bf16[96,1024]{1,0:T(8,128)(2,1)S(1)} %shard_map.74), channel_id=1, source_target_pairs={{0,1},{1,0},{2,3},{3,2},{4,5},{5,4},{6,7},{7,6},{8,9},{9,8},{10,11... | collective-permute-start | bytes 589832 | tf_op jit(solution)/shard_map/ppermute | solution.py:40
  65.7 7.9 %copy-start.4 = (f32[1,256,1024]{2,1,0:T(8,128)S(1)}, f32[1,256,1024]{2,1,0:T(8,128)}, u32[]{:S(2)}) copy-start(f32[1,256,1024]{2,1,0:T(8,128)} %param.11) | copy-start | bytes 3145732
  69.3 8.7 %collective-permute-start.14 = (bf16[80,1024]{1,0:T(8,128)(2,1)S(1)}, bf16[80,1024]{1,0:T(8,128)(2,1)S(1)}, u32[]{:S(2)}, u32[]{:S(2)}) collective-permute-start(bf16[80,1024]{1,0:T(8,128)(2,1)S(1)} %get-tuple-element.37), channel_id=1, source_target_pairs={{0,1},{1,0},{2,3},{3,2},{4,5},{5,4},{6,7},{7,6},{8,9},{9,8},{10,11... | collective-permute-start | bytes 491528 | tf_op jit(solution)/shard_map/ppermute | solution.py:40
  71.5 6.6 %collective-permute-start.15 = (bf16[80,1024]{1,0:T(8,128)(2,1)S(1)}, bf16[80,1024]{1,0:T(8,128)(2,1)S(1)}, u32[]{:S(2)}, u32[]{:S(2)}) collective-permute-start(bf16[80,1024]{1,0:T(8,128)(2,1)S(1)} %get-tuple-element.38), channel_id=1, source_target_pairs={{0,1},{1,0},{2,3},{3,2},{4,5},{5,4},{6,7},{7,6},{8,9},{9,8},{10,11... | collective-permute-start | bytes 491528 | tf_op jit(solution)/shard_map/ppermute | solution.py:40
  71.5 6.5 %collective-permute-start.13 = (bf16[96,256]{1,0:T(8,128)(2,1)S(1)}, bf16[96,256]{1,0:T(8,128)(2,1)S(1)}, u32[]{:S(2)}, u32[]{:S(2)}) collective-permute-start(bf16[96,256]{1,0:T(8,128)(2,1)S(1)} %get-tuple-element.36), channel_id=1, source_target_pairs={{0,1},{1,0},{2,3},{3,2},{4,5},{5,4},{6,7},{7,6},{8,9},{9,8},{10,11... | collective-permute-start | bytes 147464 | tf_op jit(solution)/shard_map/ppermute | solution.py:40
  73.5 4.5 %collective-permute-start.11 = (f32[8,128]{1,0:T(8,128)S(1)}, f32[8,128]{1,0:T(8,128)S(1)}, u32[]{:S(2)}, u32[]{:S(2)}) collective-permute-start(f32[8,128]{1,0:T(8,128)S(1)} %get-tuple-element.34.squares), channel_id=1, source_target_pairs={{0,1},{1,0},{2,3},{3,2},{4,5},{5,4},{6,7},{7,6},{8,9},{9,8},{10,11... | collective-permute-start | bytes 12296 | tf_op jit(solution)/shard_map/ppermute | solution.py:40
where the time goes:
time: 79.5 us; the launch traced here: 79.2 us
  waiting for transfers between devices  39.9 us (50%)
  starting transfers between devices  23.5 us (30%)
  Pallas kernels  12.6 us (16%)
  local copies, waits for them, and re-layouts  3.15 us (4%)
    ppermute x5, waiting for transfers between devices, from_peers(): lax.ppermute(value, axis, [(source, (source - step) % count) for source i...  31.8 us
    pallas_call x12, Pallas kernels, call(): pl.pallas_call(kernel, out_shape=outs, compiler_params=pltpu.CompilerPara...  12.6 us
    ppermute x5, starting transfers between devices, from_peers(): lax.ppermute(value, axis, [(source, (source - step) % count) for source i...  9.23 us
    ppermute x4, starting transfers between devices, passed_along(): lax.ppermute(value, axis, [(source, source + steps) for source in range(i...  6.63 us
    ppermute x5, starting transfers between devices, to_peer(): lax.ppermute(value, axis, [(source, (source + step) % count) for source i...  6.38 us
    ppermute x5, waiting for transfers between devices, to_peer(): lax.ppermute(value, axis, [(source, (source + step) % count) for source i...  4.23 us
    ppermute x2, waiting for transfers between devices, passed_round(): lax.ppermute(value, axis, [(source, (source + 1) % count) for source in r...  3.81 us
    unnamed x16, local copies, waits for them, and re-layouts  3.15 us
  transfers between devices with their start and end apart: 16, of which 8 were waited for; matrix products, arithmetic and copies ran while one was open for 0% of the time, Pallas kernels for 14%

commit v1 on v0

--- a/solution.py
+++ b/solution.py
@@ -226,8 +226,11 @@
                 update = nears[step][...].astype(FULL) - rest
             total += update * scales[step]
         scratch[here, :] = total
-        copies.append(pltpu.make_async_copy(scratch.at[here, :], out.at[here, :], sems.at[at]))
-        copies[-1].start()
+        if at >= PARTS - 1:
+            done = slice(nears[0].shape[0], row) if at < PARTS else here
+            sem = sems.at[at - PARTS + 1]
+            copies.append(pltpu.make_async_copy(scratch.at[done, :], out.at[done, :], sem))
+            copies[-1].start()
     for copy in copies:
         copy.wait()
 
@@ -350,7 +353,7 @@
         4 * rows * wide,
         in_specs=[pl.BlockSpec(memory_space=pltpu.VMEM)] * len(operands),
         out_specs=[anywhere],
-        scratch_shapes=[pltpu.VMEM((rows, wide), FULL), pltpu.SemaphoreType.DMA((PARTS + 1,))],
+        scratch_shapes=[pltpu.VMEM((rows, wide), FULL), pltpu.SemaphoreType.DMA((2,))],
     )
     return result[None]
 

time: 79.5 us -> 79.6 us (level)
  no operation moved by 1% of the time
where the time goes in v1:
time: 79.6 us; the launch traced here: 79.3 us
  waiting for transfers between devices  39.9 us (50%)
  starting transfers between devices  23.5 us (30%)
  Pallas kernels  12.6 us (16%)
  local copies, waits for them, and re-layouts  3.15 us (4%)
    ppermute x5, waiting for transfers between devices, from_peers(): lax.ppermute(value, axis, [(source, (source - step) % count) for source i...  31.8 us
    pallas_call x12, Pallas kernels, call(): pl.pallas_call(kernel, out_shape=outs, compiler_params=pltpu.CompilerPara...  12.6 us
    ppermute x5, starting transfers between devices, from_peers(): lax.ppermute(value, axis, [(source, (source - step) % count) for source i...  9.23 us
    ppermute x4, starting transfers between devices, passed_along(): lax.ppermute(value, axis, [(source, source + steps) for source in range(i...  6.63 us
    ppermute x5, starting transfers between devices, to_peer(): lax.ppermute(value, axis, [(source, (source + step) % count) for source i...  6.38 us
    ppermute x5, waiting for transfers between devices, to_peer(): lax.ppermute(value, axis, [(source, (source + step) % count) for source i...  4.23 us
    ppermute x2, waiting for transfers between devices, passed_round(): lax.ppermute(value, axis, [(source, (source + 1) % count) for source in r...  3.81 us
    unnamed x16, local copies, waits for them, and re-layouts  3.15 us
  transfers between devices with their start and end apart: 16, of which 8 were waited for; matrix products, arithmetic and copies ran while one was open for 0% of the time, Pallas kernels for 14%

profile of v1, /device:TPU:0, one launch (start us, length us, event | category | flops | bytes accessed | tf_op | source)
XLA Modules:
  0.0 79.3 jit_solution(17710612643222363606)
XLA Ops:
  0.0 3.0 %collective-permute-start.2 = (bf16[512,1024]{1,0:T(8,128)(2,1)}, bf16[512,1024]{1,0:T(8,128)(2,1)S(1)}, u32[]{:S(2)}, u32[]{:S(2)}) collective-permute-start(bf16[512,1024]{1,0:T(8,128)(2,1)} %bitcast.20), channel_id=1, source_target_pairs={{0,1},{1,0},{2,3},{3,2},{4,5},{5,4},{6,7},{7,6},{8,9},{9,8},{10,11... | collective-permute-start | bytes 3145736 | tf_op jit(solution)/shard_map/ppermute | solution.py:33
  3.0 1.3 %collective-permute-start = (bf16[512,1024]{1,0:T(8,128)(2,1)}, bf16[512,1024]{1,0:T(8,128)(2,1)S(1)}, u32[]{:S(2)}, u32[]{:S(2)}) collective-permute-start(bf16[512,1024]{1,0:T(8,128)(2,1)} %bitcast.18), channel_id=1, source_target_pairs={{2,0},{4,2},{6,4},{8,6},{10,8},{12,10},{14,12},{16,14},{18,16},{20... | collective-permute-start | bytes 3145736 | tf_op jit(solution)/shard_map/ppermute | solution.py:22
  4.3 0.9 %copy-done = bf16[1,256,512]{2,1,0:T(8,128)(2,1)S(1)} copy-done((bf16[1,256,512]{2,1,0:T(8,128)(2,1)S(1)}, bf16[1,256,512]{2,1,0:T(8,128)(2,1)}, u32[]{:S(2)}) %copy-start) | copy-done | bytes 262168
  5.2 1.2 %copy-done.2 = bf16[1,512,1024]{2,1,0:T(8,128)(2,1)S(1)} copy-done((bf16[1,512,1024]{2,1,0:T(8,128)(2,1)S(1)}, bf16[1,512,1024]{2,1,0:T(8,128)(2,1)}, u32[]{:S(2)}) %copy-start.2) | copy-done | bytes 1048600
  6.4 0.9 %copy-done.5 = bf16[1,256,512]{2,1,0:T(8,128)(2,1)S(1)} copy-done((bf16[1,256,512]{2,1,0:T(8,128)(2,1)S(1)}, bf16[1,256,512]{2,1,0:T(8,128)(2,1)}, u32[]{:S(2)}) %copy-start.5) | copy-done | bytes 262168
  7.7 2.0 %collective-permute-start.3 = (bf16[512,512]{1,0:T(8,128)(2,1)S(1)}, bf16[512,512]{1,0:T(8,128)(2,1)S(1)}, u32[]{:S(2)}, u32[]{:S(2)}) collective-permute-start(bf16[512,512]{1,0:T(8,128)(2,1)S(1)} %get-tuple-element.23), channel_id=1, source_target_pairs={{0,1},{1,0},{2,3},{3,2},{4,5},{5,4},{6,7},{7,6},{8,9},{9,8},{10,11... | collective-permute-start | bytes 1572872 | tf_op jit(solution)/shard_map/ppermute | solution.py:33
  9.7 2.5 %collective-permute-start.8 = (bf16[512,1024]{1,0:T(8,128)(2,1)}, bf16[512,1024]{1,0:T(8,128)(2,1)S(1)}, u32[]{:S(2)}, u32[]{:S(2)}) collective-permute-start(bf16[512,1024]{1,0:T(8,128)(2,1)} %bitcast.21), channel_id=1, source_target_pairs={{0,2},{2,4},{4,6},{6,8},{8,10},{10,12},{12,14},{14,16},{16,18},{18... | collective-permute-start | bytes 3145736 | tf_op jit(solution)/shard_map/ppermute | solution.py:22
  12.3 14.9 %collective-permute-done.2.refs_1_ = bf16[512,1024]{1,0:T(8,128)(2,1)S(1)} collective-permute-done((bf16[512,1024]{1,0:T(8,128)(2,1)}, bf16[512,1024]{1,0:T(8,128)(2,1)S(1)}, u32[]{:S(2)}, u32[]{:S(2)}) %collective-permute-start.2) | collective-permute-done | bytes 1048608 | tf_op jit(solution)/shard_map/ppermute | solution.py:33
  27.2 1.3 %collective-permute-start.9 = (bf16[512,1024]{1,0:T(8,128)(2,1)S(1)}, bf16[512,1024]{1,0:T(8,128)(2,1)S(1)}, u32[]{:S(2)}, u32[]{:S(2)}) collective-permute-start(bf16[512,1024]{1,0:T(8,128)(2,1)S(1)} %collective-permute-done.2.refs_1_), channel_id=1, source_target_pairs={{0,2},{2,4},{4,6},{6,8},{8,10},{10,12},{12,14},{14,16},{16,18},{18... | collective-permute-start | bytes 3145736 | tf_op jit(solution)/shard_map/ppermute | solution.py:22
  28.5 9.9 %collective-permute-done.1.refs_0_.refs_2_.refs_1_ = bf16[512,512]{1,0:T(8,128)(2,1)S(1)} collective-permute-done((bf16[512,512]{1,0:T(8,128)(2,1)S(1)}, bf16[512,512]{1,0:T(8,128)(2,1)S(1)}, u32[]{:S(2)}, u32[]{:S(2)}) %collective-permute-start.1) | collective-permute-done | bytes 524320 | tf_op jit(solution)/shard_map/ppermute | solution.py:33
  38.4 2.1 %collective-permute-start.4 = (bf16[512,256]{1,0:T(8,128)(2,1)S(1)}, bf16[512,256]{1,0:T(8,128)(2,1)S(1)}, u32[]{:S(2)}, u32[]{:S(2)}) collective-permute-start(bf16[512,256]{1,0:T(8,128)(2,1)S(1)} %get-tuple-element.25), channel_id=1, source_target_pairs={{0,1},{1,0},{2,3},{3,2},{4,5},{5,4},{6,7},{7,6},{8,9},{9,8},{10,11... | collective-permute-start | bytes 786440 | tf_op jit(solution)/shard_map/ppermute | solution.py:33
  40.5 1.3 %shard_map.65.first = bf16[512,1024]{1,0:T(8,128)(2,1)S(1)} custom-call(s32[1]{0:T(128)} %bitcast.1.me, bf16[512,1024]{1,0:T(8,128)(2,1)S(1)} %collective-permute-done.following, bf16[256,512]{1,0:T(8,128)(2,1)S(1)} %bitcast.9, bf16[512,512]{1,0:T(8,128)(2,1)S(1)} %collective-permute-done.1.refs_0_.refs_2_.refs_1_), custom_call_target="tpu_custom_call" | custom-call | flops 8388608 | bytes 45056 | tf_op jit(solution)/shard_map/pallas_call | solution.py:244
  41.8 3.6 %shard_map.66.left = bf16[512,1024]{1,0:T(8,128)(2,1)S(1)} custom-call(s32[1]{0:T(128)} %bitcast.1.me, bf16[512,1024]{1,0:T(8,128)(2,1)S(1)} %bitcast.19, bf16[512,1024]{1,0:T(8,128)(2,1)S(1)} %shard_map.65.first, bf16[256,512]{1,0:T(8,128)(2,1)S(1)} %bitcast.17, bf16[512,1024]{1,0:T(8,128)(2,1)S(1)} %bitcast.22, ...), custom_call_target="tpu_custom_call" | custom-call | flops 25165824 | bytes 94208 | tf_op jit(solution)/shard_map/pallas_call | solution.py:244
  45.4 1.2 %shard_map.67.mine = f32[512,1024]{1,0:T(8,128)S(1)} custom-call(s32[1]{0:T(128)} %bitcast.1.me, bf16[512,1024]{1,0:T(8,128)(2,1)S(1)} %shard_map.66.left, bf16[512,1024]{1,0:T(8,128)(2,1)S(1)} %bitcast.14), custom_call_target="tpu_custom_call" | custom-call | flops 8388608 | bytes 65536 | tf_op jit(solution)/shard_map/pallas_call | solution.py:244
  46.6 3.0 %collective-permute-done.3.refs_0_ = bf16[512,512]{1,0:T(8,128)(2,1)S(1)} collective-permute-done((bf16[512,512]{1,0:T(8,128)(2,1)S(1)}, bf16[512,512]{1,0:T(8,128)(2,1)S(1)}, u32[]{:S(2)}, u32[]{:S(2)}) %collective-permute-start.3) | collective-permute-done | bytes 524320 | tf_op jit(solution)/shard_map/ppermute | solution.py:33
  49.6 0.9 %shard_map.68 = (bf16[512,512]{1,0:T(8,128)(2,1)S(1)}, bf16[512,512]{1,0:T(8,128)(2,1)S(1)}) custom-call(s32[1]{0:T(128)} %bitcast.1.me, bf16[512,1024]{1,0:T(8,128)(2,1)S(1)} %shard_map.66.left, f32[512,1024]{1,0:T(8,128)S(1)} %shard_map.67.mine, bf16[256,512]{1,0:T(8,128)(2,1)S(1)} %bitcast.10, bf16[512,512]{1,0:T(8,128)(2,1)S(1)} %collective-permute-done.3.refs_0_, ...), custom_call_target="tpu_custom_call" | custom-call | flops 12582912 | bytes 86016 | tf_op jit(solution)/shard_map/pallas_call | solution.py:244
  50.6 2.1 %collective-permute-start.5 = (bf16[512,256]{1,0:T(8,128)(2,1)S(1)}, bf16[512,256]{1,0:T(8,128)(2,1)S(1)}, u32[]{:S(2)}, u32[]{:S(2)}) collective-permute-start(bf16[512,256]{1,0:T(8,128)(2,1)S(1)} %get-tuple-element.27), channel_id=1, source_target_pairs={{0,1},{1,0},{2,3},{3,2},{4,5},{5,4},{6,7},{7,6},{8,9},{9,8},{10,11... | collective-permute-start | bytes 786440 | tf_op jit(solution)/shard_map/ppermute | solution.py:33
  52.7 1.7 %collective-permute-done.4.refs_0_ = bf16[512,256]{1,0:T(8,128)(2,1)S(1)} collective-permute-done((bf16[512,256]{1,0:T(8,128)(2,1)S(1)}, bf16[512,256]{1,0:T(8,128)(2,1)S(1)}, u32[]{:S(2)}, u32[]{:S(2)}) %collective-permute-start.4) | collective-permute-done | bytes 262176 | tf_op jit(solution)/shard_map/ppermute | solution.py:33
  54.4 0.8 %shard_map.69 = (bf16[512,256]{1,0:T(8,128)(2,1)S(1)}, bf16[512,256]{1,0:T(8,128)(2,1)S(1)}) custom-call(s32[1]{0:T(128)} %bitcast.1.me, bf16[512,1024]{1,0:T(8,128)(2,1)S(1)} %shard_map.66.left, f32[512,1024]{1,0:T(8,128)S(1)} %shard_map.67.mine, bf16[256,512]{1,0:T(8,128)(2,1)S(1)} %bitcast.11, bf16[512,256]{1,0:T(8,128)(2,1)S(1)} %collective-permute-done.4.refs_0_, ...), custom_call_target="tpu_custom_call" | custom-call | flops 6291456 | bytes 73728 | tf_op jit(solution)/shard_map/pallas_call | solution.py:244
  55.3 1.5 %collective-permute-start.7 = (bf16[512,256]{1,0:T(8,128)(2,1)S(1)}, bf16[512,256]{1,0:T(8,128)(2,1)S(1)}, u32[]{:S(2)}, u32[]{:S(2)}) collective-permute-start(bf16[512,256]{1,0:T(8,128)(2,1)S(1)} %get-tuple-element.30), channel_id=1, source_target_pairs={{0,2},{2,4},{4,6},{6,8},{8,10},{10,12},{12,14},{14,16},{16,18},{18... | collective-permute-start | bytes 786440 | tf_op jit(solution)/shard_map/ppermute | solution.py:22
  56.8 2.3 %collective-permute-done.5.refs_0_ = bf16[512,256]{1,0:T(8,128)(2,1)S(1)} collective-permute-done((bf16[512,256]{1,0:T(8,128)(2,1)S(1)}, bf16[512,256]{1,0:T(8,128)(2,1)S(1)}, u32[]{:S(2)}, u32[]{:S(2)}) %collective-permute-start.5) | collective-permute-done | bytes 262176 | tf_op jit(solution)/shard_map/ppermute | solution.py:33
  59.1 0.8 %shard_map.70 = (bf16[512,256]{1,0:T(8,128)(2,1)S(1)}, bf16[512,256]{1,0:T(8,128)(2,1)S(1)}) custom-call(s32[1]{0:T(128)} %bitcast.1.me, bf16[512,1024]{1,0:T(8,128)(2,1)S(1)} %shard_map.66.left, f32[512,1024]{1,0:T(8,128)S(1)} %shard_map.67.mine, bf16[256,512]{1,0:T(8,128)(2,1)S(1)} %bitcast.12, bf16[512,256]{1,0:T(8,128)(2,1)S(1)} %collective-permute-done.5.refs_0_, ...), custom_call_target="tpu_custom_call" | custom-call | flops 6291456 | bytes 73728 | tf_op jit(solution)/shard_map/pallas_call | solution.py:244
  59.9 1.2 %collective-permute-start.10 = (bf16[512,256]{1,0:T(8,128)(2,1)S(1)}, bf16[512,256]{1,0:T(8,128)(2,1)S(1)}, u32[]{:S(2)}, u32[]{:S(2)}) collective-permute-start(bf16[512,256]{1,0:T(8,128)(2,1)S(1)} %get-tuple-element.33), channel_id=1, source_target_pairs={{0,2},{2,4},{4,6},{6,8},{8,10},{10,12},{12,14},{14,16},{16,18},{18... | collective-permute-start | bytes 786440 | tf_op jit(solution)/shard_map/ppermute | solution.py:27
  61.1 0.8 %collective-permute-done.6.refs_3_ = bf16[512,512]{1,0:T(8,128)(2,1)S(1)} collective-permute-done((bf16[512,512]{1,0:T(8,128)(2,1)S(1)}, bf16[512,512]{1,0:T(8,128)(2,1)S(1)}, u32[]{:S(2)}, u32[]{:S(2)}) %collective-permute-start.6) | collective-permute-done | bytes 524320 | tf_op jit(solution)/shard_map/ppermute | solution.py:27
  61.9 0.6 shard_map.74
  62.5 2.1 %collective-permute-start.12 = (bf16[96,1024]{1,0:T(8,128)(2,1)S(1)}, bf16[96,1024]{1,0:T(8,128)(2,1)S(1)}, u32[]{:S(2)}, u32[]{:S(2)}) collective-permute-start(bf16[96,1024]{1,0:T(8,128)(2,1)S(1)} %shard_map.74), channel_id=1, source_target_pairs={{0,1},{1,0},{2,3},{3,2},{4,5},{5,4},{6,7},{7,6},{8,9},{9,8},{10,11... | collective-permute-start | bytes 589832 | tf_op jit(solution)/shard_map/ppermute | solution.py:40
  64.6 1.1 %shard_map.71 = (f32[512,1024]{1,0:T(8,128)S(1)}, bf16[1024,256]{1,0:T(8,128)(2,1)S(1)}) custom-call(s32[1]{0:T(128)} %bitcast.1.me, bf16[512,512]{1,0:T(8,128)(2,1)S(1)} %get-tuple-element.24.refs_0_, bf16[512,256]{1,0:T(8,128)(2,1)S(1)} %get-tuple-element.26.refs_1_, bf16[512,256]{1,0:T(8,128)(2,1)S(1)} %get-tuple-element.28.refs_2_, ...), custom_call_target="tpu_custom_call" | custom-call | flops 805306368 | bytes 102400 | tf_op jit(solution)/shard_map/pallas_call | solution.py:244
  65.7 3.0 %collective-permute-done.10.refs_0_ = bf16[512,256]{1,0:T(8,128)(2,1)S(1)} collective-permute-done((bf16[512,256]{1,0:T(8,128)(2,1)S(1)}, bf16[512,256]{1,0:T(8,128)(2,1)S(1)}, u32[]{:S(2)}, u32[]{:S(2)}) %collective-permute-start.10) | collective-permute-done | bytes 262176 | tf_op jit(solution)/shard_map/ppermute | solution.py:27
  69.3 2.2 %collective-permute-start.14 = (bf16[80,1024]{1,0:T(8,128)(2,1)S(1)}, bf16[80,1024]{1,0:T(8,128)(2,1)S(1)}, u32[]{:S(2)}, u32[]{:S(2)}) collective-permute-start(bf16[80,1024]{1,0:T(8,128)(2,1)S(1)} %get-tuple-element.37), channel_id=1, source_target_pairs={{0,1},{1,0},{2,3},{3,2},{4,5},{5,4},{6,7},{7,6},{8,9},{9,8},{10,11... | collective-permute-start | bytes 491528 | tf_op jit(solution)/shard_map/ppermute | solution.py:40
  71.5 1.9 %collective-permute-start.13 = (bf16[96,256]{1,0:T(8,128)(2,1)S(1)}, bf16[96,256]{1,0:T(8,128)(2,1)S(1)}, u32[]{:S(2)}, u32[]{:S(2)}) collective-permute-start(bf16[96,256]{1,0:T(8,128)(2,1)S(1)} %get-tuple-element.36), channel_id=1, source_target_pairs={{0,1},{1,0},{2,3},{3,2},{4,5},{5,4},{6,7},{7,6},{8,9},{9,8},{10,11... | collective-permute-start | bytes 147464 | tf_op jit(solution)/shard_map/ppermute | solution.py:40
  73.8 4.2 %collective-permute-done.11.refs_0_ = f32[8,128]{1,0:T(8,128)S(1)} collective-permute-done((f32[8,128]{1,0:T(8,128)S(1)}, f32[8,128]{1,0:T(8,128)S(1)}, u32[]{:S(2)}, u32[]{:S(2)}) %collective-permute-start.11) | collective-permute-done | bytes 4128 | tf_op jit(solution)/shard_map/ppermute | solution.py:40
  78.1 1.2 %shard_map.75 = f32[256,1024]{1,0:T(8,128)} custom-call(f32[256,1024]{1,0:T(8,128)S(1)} %shard_map.73.base, bf16[1024,256]{1,0:T(8,128)(2,1)S(1)} %get-tuple-element.32.right_rest, f32[8,128]{1,0:T(8,128)S(1)} %collective-permute-done.11.refs_0_, bf16[96,1024]{1,0:T(8,128)(2,1)S(1)} %collective-permute-done.12.refs_1_, ...), custom_call_target="tpu_custom_call" | custom-call | flops 1048576 | bytes 49984 | tf_op jit(solution)/shard_map/pallas_call | solution.py:244
  (28 shorter events, 1.4 us)
Async XLA Ops:
  0.0 27.2 %collective-permute-start.2 = (bf16[512,1024]{1,0:T(8,128)(2,1)}, bf16[512,1024]{1,0:T(8,128)(2,1)S(1)}, u32[]{:S(2)}, u32[]{:S(2)}) collective-permute-start(bf16[512,1024]{1,0:T(8,128)(2,1)} %bitcast.20), channel_id=1, source_target_pairs={{0,1},{1,0},{2,3},{3,2},{4,5},{5,4},{6,7},{7,6},{8,9},{9,8},{10,11... | collective-permute-start | bytes 3145736 | tf_op jit(solution)/shard_map/ppermute | solution.py:33
  3.0 37.5 %collective-permute-start = (bf16[512,1024]{1,0:T(8,128)(2,1)}, bf16[512,1024]{1,0:T(8,128)(2,1)S(1)}, u32[]{:S(2)}, u32[]{:S(2)}) collective-permute-start(bf16[512,1024]{1,0:T(8,128)(2,1)} %bitcast.18), channel_id=1, source_target_pairs={{2,0},{4,2},{6,4},{8,6},{10,8},{12,10},{14,12},{16,14},{18,16},{20... | collective-permute-start | bytes 3145736 | tf_op jit(solution)/shard_map/ppermute | solution.py:22
  4.3 1.0 %copy-start = (bf16[1,256,512]{2,1,0:T(8,128)(2,1)S(1)}, bf16[1,256,512]{2,1,0:T(8,128)(2,1)}, u32[]{:S(2)}) copy-start(bf16[1,256,512]{2,1,0:T(8,128)(2,1)} %param.9) | copy-start | bytes 786436
  5.2 1.2 %copy-start.2 = (bf16[1,512,1024]{2,1,0:T(8,128)(2,1)S(1)}, bf16[1,512,1024]{2,1,0:T(8,128)(2,1)}, u32[]{:S(2)}) copy-start(bf16[1,512,1024]{2,1,0:T(8,128)(2,1)} %param.8) | copy-start | bytes 3145732
  6.4 0.9 %copy-start.5 = (bf16[1,256,512]{2,1,0:T(8,128)(2,1)S(1)}, bf16[1,256,512]{2,1,0:T(8,128)(2,1)}, u32[]{:S(2)}) copy-start(bf16[1,256,512]{2,1,0:T(8,128)(2,1)} %param.7) | copy-start | bytes 786436
  7.4 34.4 %copy-start.6 = (bf16[1,1,512,1024]{3,2,1,0:T(8,128)(2,1)S(1)}, bf16[1,1,512,1024]{3,2,1,0:T(8,128)(2,1)}, u32[]{:S(2)}) copy-start(bf16[1,1,512,1024]{3,2,1,0:T(8,128)(2,1)} %param.6) | copy-start | bytes 3145732
  7.4 34.4 %copy-start.7 = (bf16[1,512,1024]{2,1,0:T(8,128)(2,1)S(1)}, bf16[1,512,1024]{2,1,0:T(8,128)(2,1)}, u32[]{:S(2)}) copy-start(bf16[1,512,1024]{2,1,0:T(8,128)(2,1)} %param.10) | copy-start | bytes 3145732
  7.6 30.8 %collective-permute-start.1 = (bf16[512,512]{1,0:T(8,128)(2,1)S(1)}, bf16[512,512]{1,0:T(8,128)(2,1)S(1)}, u32[]{:S(2)}, u32[]{:S(2)}) collective-permute-start(bf16[512,512]{1,0:T(8,128)(2,1)S(1)} %get-tuple-element.22), channel_id=1, source_target_pairs={{0,1},{1,0},{2,3},{3,2},{4,5},{5,4},{6,7},{7,6},{8,9},{9,8},{10,11... | collective-permute-start | bytes 1572872 | tf_op jit(solution)/shard_map/ppermute | solution.py:33
  7.7 41.9 %collective-permute-start.3 = (bf16[512,512]{1,0:T(8,128)(2,1)S(1)}, bf16[512,512]{1,0:T(8,128)(2,1)S(1)}, u32[]{:S(2)}, u32[]{:S(2)}) collective-permute-start(bf16[512,512]{1,0:T(8,128)(2,1)S(1)} %get-tuple-element.23), channel_id=1, source_target_pairs={{0,1},{1,0},{2,3},{3,2},{4,5},{5,4},{6,7},{7,6},{8,9},{9,8},{10,11... | collective-permute-start | bytes 1572872 | tf_op jit(solution)/shard_map/ppermute | solution.py:33
  9.7 51.3 %collective-permute-start.8 = (bf16[512,1024]{1,0:T(8,128)(2,1)}, bf16[512,1024]{1,0:T(8,128)(2,1)S(1)}, u32[]{:S(2)}, u32[]{:S(2)}) collective-permute-start(bf16[512,1024]{1,0:T(8,128)(2,1)} %bitcast.21), channel_id=1, source_target_pairs={{0,2},{2,4},{4,6},{6,8},{8,10},{10,12},{12,14},{14,16},{16,18},{18... | collective-permute-start | bytes 3145736 | tf_op jit(solution)/shard_map/ppermute | solution.py:22
  27.2 34.7 %collective-permute-start.9 = (bf16[512,1024]{1,0:T(8,128)(2,1)S(1)}, bf16[512,1024]{1,0:T(8,128)(2,1)S(1)}, u32[]{:S(2)}, u32[]{:S(2)}) collective-permute-start(bf16[512,1024]{1,0:T(8,128)(2,1)S(1)} %collective-permute-done.2.refs_1_), channel_id=1, source_target_pairs={{0,2},{2,4},{4,6},{6,8},{8,10},{10,12},{12,14},{14,16},{16,18},{18... | collective-permute-start | bytes 3145736 | tf_op jit(solution)/shard_map/ppermute | solution.py:22
  38.4 16.0 %collective-permute-start.4 = (bf16[512,256]{1,0:T(8,128)(2,1)S(1)}, bf16[512,256]{1,0:T(8,128)(2,1)S(1)}, u32[]{:S(2)}, u32[]{:S(2)}) collective-permute-start(bf16[512,256]{1,0:T(8,128)(2,1)S(1)} %get-tuple-element.25), channel_id=1, source_target_pairs={{0,1},{1,0},{2,3},{3,2},{4,5},{5,4},{6,7},{7,6},{8,9},{9,8},{10,11... | collective-permute-start | bytes 786440 | tf_op jit(solution)/shard_map/ppermute | solution.py:33
  41.8 3.6 %copy-start.3 = (bf16[1,512,1024]{2,1,0:T(8,128)(2,1)S(1)}, bf16[1,512,1024]{2,1,0:T(8,128)(2,1)}, u32[]{:S(2)}) copy-start(bf16[1,512,1024]{2,1,0:T(8,128)(2,1)} %param.8) | copy-start | bytes 3145732
  45.4 4.3 %copy-start.1 = (bf16[1,256,512]{2,1,0:T(8,128)(2,1)S(1)}, bf16[1,256,512]{2,1,0:T(8,128)(2,1)}, u32[]{:S(2)}) copy-start(bf16[1,256,512]{2,1,0:T(8,128)(2,1)} %param.9) | copy-start | bytes 786436
  50.5 11.4 %collective-permute-start.6 = (bf16[512,512]{1,0:T(8,128)(2,1)S(1)}, bf16[512,512]{1,0:T(8,128)(2,1)S(1)}, u32[]{:S(2)}, u32[]{:S(2)}) collective-permute-start(bf16[512,512]{1,0:T(8,128)(2,1)S(1)} %get-tuple-element.29), channel_id=1, source_target_pairs={{0,2},{2,4},{4,6},{6,8},{8,10},{10,12},{12,14},{14,16},{16,18},{18... | collective-permute-start | bytes 1572872 | tf_op jit(solution)/shard_map/ppermute | solution.py:27
  50.6 8.4 %collective-permute-start.5 = (bf16[512,256]{1,0:T(8,128)(2,1)S(1)}, bf16[512,256]{1,0:T(8,128)(2,1)S(1)}, u32[]{:S(2)}, u32[]{:S(2)}) collective-permute-start(bf16[512,256]{1,0:T(8,128)(2,1)S(1)} %get-tuple-element.27), channel_id=1, source_target_pairs={{0,1},{1,0},{2,3},{3,2},{4,5},{5,4},{6,7},{7,6},{8,9},{9,8},{10,11... | collective-permute-start | bytes 786440 | tf_op jit(solution)/shard_map/ppermute | solution.py:33
  55.3 5.8 %collective-permute-start.7 = (bf16[512,256]{1,0:T(8,128)(2,1)S(1)}, bf16[512,256]{1,0:T(8,128)(2,1)S(1)}, u32[]{:S(2)}, u32[]{:S(2)}) collective-permute-start(bf16[512,256]{1,0:T(8,128)(2,1)S(1)} %get-tuple-element.30), channel_id=1, source_target_pairs={{0,2},{2,4},{4,6},{6,8},{8,10},{10,12},{12,14},{14,16},{16,18},{18... | collective-permute-start | bytes 786440 | tf_op jit(solution)/shard_map/ppermute | solution.py:22
  59.9 8.8 %collective-permute-start.10 = (bf16[512,256]{1,0:T(8,128)(2,1)S(1)}, bf16[512,256]{1,0:T(8,128)(2,1)S(1)}, u32[]{:S(2)}, u32[]{:S(2)}) collective-permute-start(bf16[512,256]{1,0:T(8,128)(2,1)S(1)} %get-tuple-element.33), channel_id=1, source_target_pairs={{0,2},{2,4},{4,6},{6,8},{8,10},{10,12},{12,14},{14,16},{16,18},{18... | collective-permute-start | bytes 786440 | tf_op jit(solution)/shard_map/ppermute | solution.py:27
  62.5 15.5 %collective-permute-start.12 = (bf16[96,1024]{1,0:T(8,128)(2,1)S(1)}, bf16[96,1024]{1,0:T(8,128)(2,1)S(1)}, u32[]{:S(2)}, u32[]{:S(2)}) collective-permute-start(bf16[96,1024]{1,0:T(8,128)(2,1)S(1)} %shard_map.74), channel_id=1, source_target_pairs={{0,1},{1,0},{2,3},{3,2},{4,5},{5,4},{6,7},{7,6},{8,9},{9,8},{10,11... | collective-permute-start | bytes 589832 | tf_op jit(solution)/shard_map/ppermute | solution.py:40
  65.7 7.9 %copy-start.4 = (f32[1,256,1024]{2,1,0:T(8,128)S(1)}, f32[1,256,1024]{2,1,0:T(8,128)}, u32[]{:S(2)}) copy-start(f32[1,256,1024]{2,1,0:T(8,128)} %param.11) | copy-start | bytes 3145732
  69.3 8.7 %collective-permute-start.14 = (bf16[80,1024]{1,0:T(8,128)(2,1)S(1)}, bf16[80,1024]{1,0:T(8,128)(2,1)S(1)}, u32[]{:S(2)}, u32[]{:S(2)}) collective-permute-start(bf16[80,1024]{1,0:T(8,128)(2,1)S(1)} %get-tuple-element.37), channel_id=1, source_target_pairs={{0,1},{1,0},{2,3},{3,2},{4,5},{5,4},{6,7},{7,6},{8,9},{9,8},{10,11... | collective-permute-start | bytes 491528 | tf_op jit(solution)/shard_map/ppermute | solution.py:40
  71.5 6.6 %collective-permute-start.15 = (bf16[80,1024]{1,0:T(8,128)(2,1)S(1)}, bf16[80,1024]{1,0:T(8,128)(2,1)S(1)}, u32[]{:S(2)}, u32[]{:S(2)}) collective-permute-start(bf16[80,1024]{1,0:T(8,128)(2,1)S(1)} %get-tuple-element.38), channel_id=1, source_target_pairs={{0,1},{1,0},{2,3},{3,2},{4,5},{5,4},{6,7},{7,6},{8,9},{9,8},{10,11... | collective-permute-start | bytes 491528 | tf_op jit(solution)/shard_map/ppermute | solution.py:40
  71.5 6.5 %collective-permute-start.13 = (bf16[96,256]{1,0:T(8,128)(2,1)S(1)}, bf16[96,256]{1,0:T(8,128)(2,1)S(1)}, u32[]{:S(2)}, u32[]{:S(2)}) collective-permute-start(bf16[96,256]{1,0:T(8,128)(2,1)S(1)} %get-tuple-element.36), channel_id=1, source_target_pairs={{0,1},{1,0},{2,3},{3,2},{4,5},{5,4},{6,7},{7,6},{8,9},{9,8},{10,11... | collective-permute-start | bytes 147464 | tf_op jit(solution)/shard_map/ppermute | solution.py:40
  73.5 4.5 %collective-permute-start.11 = (f32[8,128]{1,0:T(8,128)S(1)}, f32[8,128]{1,0:T(8,128)S(1)}, u32[]{:S(2)}, u32[]{:S(2)}) collective-permute-start(f32[8,128]{1,0:T(8,128)S(1)} %get-tuple-element.34.squares), channel_id=1, source_target_pairs={{0,1},{1,0},{2,3},{3,2},{4,5},{5,4},{6,7},{7,6},{8,9},{9,8},{10,11... | collective-permute-start | bytes 12296 | tf_op jit(solution)/shard_map/ppermute | solution.py:40

commit v2 on v0

--- a/solution.py
+++ b/solution.py
@@ -303,7 +303,7 @@
         preconds.append(precond)
         ring = at != 1
         backs.append(passed_round(back, "layer") if ring else passed_along(back, "layer", 1))
-    near = 3 * rows // 8 // ROWS * ROWS
+    near = 7 * rows // 16 // ROWS * ROWS
     peers, last, later = count - 1, widths[-1], sum(widths[EARLY:])
     far_rows, left_rows = [], rows - near
     for at in range(PARTS, 0, -1):

time: 79.5 us -> 79.7 us (level)
  no operation moved by 1% of the time
where the time goes in v2:
time: 79.7 us; the launch traced here: 79.4 us
  waiting for transfers between devices  40.1 us (50%)
  starting transfers between devices  23.5 us (29%)
  Pallas kernels  12.5 us (16%)
  local copies, waits for them, and re-layouts  3.15 us (4%)
    ppermute x5, waiting for transfers between devices, from_peers(): lax.ppermute(value, axis, [(source, (source - step) % count) for source i...  31.8 us
    pallas_call x12, Pallas kernels, call(): pl.pallas_call(kernel, out_shape=outs, compiler_params=pltpu.CompilerPara...  12.5 us
    ppermute x5, starting transfers between devices, from_peers(): lax.ppermute(value, axis, [(source, (source - step) % count) for source i...  9.23 us
    ppermute x4, starting transfers between devices, passed_along(): lax.ppermute(value, axis, [(source, source + steps) for source in range(i...  6.63 us
    ppermute x5, starting transfers between devices, to_peer(): lax.ppermute(value, axis, [(source, (source + step) % count) for source i...  6.38 us
    ppermute x5, waiting for transfers between devices, to_peer(): lax.ppermute(value, axis, [(source, (source + step) % count) for source i...  4.44 us
    ppermute x2, waiting for transfers between devices, passed_round(): lax.ppermute(value, axis, [(source, (source + 1) % count) for source in r...  3.8 us
    unnamed x16, local copies, waits for them, and re-layouts  3.15 us
  transfers between devices with their start and end apart: 16, of which 8 were waited for; matrix products, arithmetic and copies ran while one was open for 0% of the time, Pallas kernels for 14%

profile of v2, /device:TPU:0, one launch (start us, length us, event | category | flops | bytes accessed | tf_op | source)
XLA Modules:
  0.0 79.4 jit_solution(380095514558473347)
XLA Ops:
  0.0 3.0 %collective-permute-start.2 = (bf16[512,1024]{1,0:T(8,128)(2,1)}, bf16[512,1024]{1,0:T(8,128)(2,1)S(1)}, u32[]{:S(2)}, u32[]{:S(2)}) collective-permute-start(bf16[512,1024]{1,0:T(8,128)(2,1)} %bitcast.20), channel_id=1, source_target_pairs={{0,1},{1,0},{2,3},{3,2},{4,5},{5,4},{6,7},{7,6},{8,9},{9,8},{10,11... | collective-permute-start | bytes 3145736 | tf_op jit(solution)/shard_map/ppermute | solution.py:33
  3.0 1.3 %collective-permute-start = (bf16[512,1024]{1,0:T(8,128)(2,1)}, bf16[512,1024]{1,0:T(8,128)(2,1)S(1)}, u32[]{:S(2)}, u32[]{:S(2)}) collective-permute-start(bf16[512,1024]{1,0:T(8,128)(2,1)} %bitcast.18), channel_id=1, source_target_pairs={{2,0},{4,2},{6,4},{8,6},{10,8},{12,10},{14,12},{16,14},{18,16},{20... | collective-permute-start | bytes 3145736 | tf_op jit(solution)/shard_map/ppermute | solution.py:22
  4.3 0.9 %copy-done = bf16[1,256,512]{2,1,0:T(8,128)(2,1)S(1)} copy-done((bf16[1,256,512]{2,1,0:T(8,128)(2,1)S(1)}, bf16[1,256,512]{2,1,0:T(8,128)(2,1)}, u32[]{:S(2)}) %copy-start) | copy-done | bytes 262168
  5.2 1.2 %copy-done.2 = bf16[1,512,1024]{2,1,0:T(8,128)(2,1)S(1)} copy-done((bf16[1,512,1024]{2,1,0:T(8,128)(2,1)S(1)}, bf16[1,512,1024]{2,1,0:T(8,128)(2,1)}, u32[]{:S(2)}) %copy-start.2) | copy-done | bytes 1048600
  6.4 0.9 %copy-done.5 = bf16[1,256,512]{2,1,0:T(8,128)(2,1)S(1)} copy-done((bf16[1,256,512]{2,1,0:T(8,128)(2,1)S(1)}, bf16[1,256,512]{2,1,0:T(8,128)(2,1)}, u32[]{:S(2)}) %copy-start.5) | copy-done | bytes 262168
  7.7 2.0 %collective-permute-start.3 = (bf16[512,512]{1,0:T(8,128)(2,1)S(1)}, bf16[512,512]{1,0:T(8,128)(2,1)S(1)}, u32[]{:S(2)}, u32[]{:S(2)}) collective-permute-start(bf16[512,512]{1,0:T(8,128)(2,1)S(1)} %get-tuple-element.23), channel_id=1, source_target_pairs={{0,1},{1,0},{2,3},{3,2},{4,5},{5,4},{6,7},{7,6},{8,9},{9,8},{10,11... | collective-permute-start | bytes 1572872 | tf_op jit(solution)/shard_map/ppermute | solution.py:33
  9.7 2.5 %collective-permute-start.8 = (bf16[512,1024]{1,0:T(8,128)(2,1)}, bf16[512,1024]{1,0:T(8,128)(2,1)S(1)}, u32[]{:S(2)}, u32[]{:S(2)}) collective-permute-start(bf16[512,1024]{1,0:T(8,128)(2,1)} %bitcast.21), channel_id=1, source_target_pairs={{0,2},{2,4},{4,6},{6,8},{8,10},{10,12},{12,14},{14,16},{16,18},{18... | collective-permute-start | bytes 3145736 | tf_op jit(solution)/shard_map/ppermute | solution.py:22
  12.3 14.9 %collective-permute-done.2.refs_1_ = bf16[512,1024]{1,0:T(8,128)(2,1)S(1)} collective-permute-done((bf16[512,1024]{1,0:T(8,128)(2,1)}, bf16[512,1024]{1,0:T(8,128)(2,1)S(1)}, u32[]{:S(2)}, u32[]{:S(2)}) %collective-permute-start.2) | collective-permute-done | bytes 1048608 | tf_op jit(solution)/shard_map/ppermute | solution.py:33
  27.2 1.3 %collective-permute-start.9 = (bf16[512,1024]{1,0:T(8,128)(2,1)S(1)}, bf16[512,1024]{1,0:T(8,128)(2,1)S(1)}, u32[]{:S(2)}, u32[]{:S(2)}) collective-permute-start(bf16[512,1024]{1,0:T(8,128)(2,1)S(1)} %collective-permute-done.2.refs_1_), channel_id=1, source_target_pairs={{0,2},{2,4},{4,6},{6,8},{8,10},{10,12},{12,14},{14,16},{16,18},{18... | collective-permute-start | bytes 3145736 | tf_op jit(solution)/shard_map/ppermute | solution.py:22
  28.5 9.9 %collective-permute-done.1.refs_0_.refs_2_.refs_1_ = bf16[512,512]{1,0:T(8,128)(2,1)S(1)} collective-permute-done((bf16[512,512]{1,0:T(8,128)(2,1)S(1)}, bf16[512,512]{1,0:T(8,128)(2,1)S(1)}, u32[]{:S(2)}, u32[]{:S(2)}) %collective-permute-start.1) | collective-permute-done | bytes 524320 | tf_op jit(solution)/shard_map/ppermute | solution.py:33
  38.4 2.1 %collective-permute-start.4 = (bf16[512,256]{1,0:T(8,128)(2,1)S(1)}, bf16[512,256]{1,0:T(8,128)(2,1)S(1)}, u32[]{:S(2)}, u32[]{:S(2)}) collective-permute-start(bf16[512,256]{1,0:T(8,128)(2,1)S(1)} %get-tuple-element.25), channel_id=1, source_target_pairs={{0,1},{1,0},{2,3},{3,2},{4,5},{5,4},{6,7},{7,6},{8,9},{9,8},{10,11... | collective-permute-start | bytes 786440 | tf_op jit(solution)/shard_map/ppermute | solution.py:33
  40.5 1.3 %shard_map.65.first = bf16[512,1024]{1,0:T(8,128)(2,1)S(1)} custom-call(s32[1]{0:T(128)} %bitcast.1.me, bf16[512,1024]{1,0:T(8,128)(2,1)S(1)} %collective-permute-done.following, bf16[256,512]{1,0:T(8,128)(2,1)S(1)} %bitcast.9, bf16[512,512]{1,0:T(8,128)(2,1)S(1)} %collective-permute-done.1.refs_0_.refs_2_.refs_1_), custom_call_target="tpu_custom_call" | custom-call | flops 8388608 | bytes 45056 | tf_op jit(solution)/shard_map/pallas_call | solution.py:241
  41.8 3.6 %shard_map.66.left = bf16[512,1024]{1,0:T(8,128)(2,1)S(1)} custom-call(s32[1]{0:T(128)} %bitcast.1.me, bf16[512,1024]{1,0:T(8,128)(2,1)S(1)} %bitcast.19, bf16[512,1024]{1,0:T(8,128)(2,1)S(1)} %shard_map.65.first, bf16[256,512]{1,0:T(8,128)(2,1)S(1)} %bitcast.17, bf16[512,1024]{1,0:T(8,128)(2,1)S(1)} %bitcast.22, ...), custom_call_target="tpu_custom_call" | custom-call | flops 25165824 | bytes 94208 | tf_op jit(solution)/shard_map/pallas_call | solution.py:241
  45.4 1.2 %shard_map.67.mine = f32[512,1024]{1,0:T(8,128)S(1)} custom-call(s32[1]{0:T(128)} %bitcast.1.me, bf16[512,1024]{1,0:T(8,128)(2,1)S(1)} %shard_map.66.left, bf16[512,1024]{1,0:T(8,128)(2,1)S(1)} %bitcast.14), custom_call_target="tpu_custom_call" | custom-call | flops 8388608 | bytes 65536 | tf_op jit(solution)/shard_map/pallas_call | solution.py:241
  46.6 3.0 %collective-permute-done.3.refs_0_ = bf16[512,512]{1,0:T(8,128)(2,1)S(1)} collective-permute-done((bf16[512,512]{1,0:T(8,128)(2,1)S(1)}, bf16[512,512]{1,0:T(8,128)(2,1)S(1)}, u32[]{:S(2)}, u32[]{:S(2)}) %collective-permute-start.3) | collective-permute-done | bytes 524320 | tf_op jit(solution)/shard_map/ppermute | solution.py:33
  49.6 0.9 %shard_map.68 = (bf16[512,512]{1,0:T(8,128)(2,1)S(1)}, bf16[512,512]{1,0:T(8,128)(2,1)S(1)}) custom-call(s32[1]{0:T(128)} %bitcast.1.me, bf16[512,1024]{1,0:T(8,128)(2,1)S(1)} %shard_map.66.left, f32[512,1024]{1,0:T(8,128)S(1)} %shard_map.67.mine, bf16[256,512]{1,0:T(8,128)(2,1)S(1)} %bitcast.10, bf16[512,512]{1,0:T(8,128)(2,1)S(1)} %collective-permute-done.3.refs_0_, ...), custom_call_target="tpu_custom_call" | custom-call | flops 12582912 | bytes 86016 | tf_op jit(solution)/shard_map/pallas_call | solution.py:241
  50.6 2.1 %collective-permute-start.5 = (bf16[512,256]{1,0:T(8,128)(2,1)S(1)}, bf16[512,256]{1,0:T(8,128)(2,1)S(1)}, u32[]{:S(2)}, u32[]{:S(2)}) collective-permute-start(bf16[512,256]{1,0:T(8,128)(2,1)S(1)} %get-tuple-element.27), channel_id=1, source_target_pairs={{0,1},{1,0},{2,3},{3,2},{4,5},{5,4},{6,7},{7,6},{8,9},{9,8},{10,11... | collective-permute-start | bytes 786440 | tf_op jit(solution)/shard_map/ppermute | solution.py:33
  52.7 1.7 %collective-permute-done.4.refs_0_ = bf16[512,256]{1,0:T(8,128)(2,1)S(1)} collective-permute-done((bf16[512,256]{1,0:T(8,128)(2,1)S(1)}, bf16[512,256]{1,0:T(8,128)(2,1)S(1)}, u32[]{:S(2)}, u32[]{:S(2)}) %collective-permute-start.4) | collective-permute-done | bytes 262176 | tf_op jit(solution)/shard_map/ppermute | solution.py:33
  54.4 0.8 %shard_map.69 = (bf16[512,256]{1,0:T(8,128)(2,1)S(1)}, bf16[512,256]{1,0:T(8,128)(2,1)S(1)}) custom-call(s32[1]{0:T(128)} %bitcast.1.me, bf16[512,1024]{1,0:T(8,128)(2,1)S(1)} %shard_map.66.left, f32[512,1024]{1,0:T(8,128)S(1)} %shard_map.67.mine, bf16[256,512]{1,0:T(8,128)(2,1)S(1)} %bitcast.11, bf16[512,256]{1,0:T(8,128)(2,1)S(1)} %collective-permute-done.4.refs_0_, ...), custom_call_target="tpu_custom_call" | custom-call | flops 6291456 | bytes 73728 | tf_op jit(solution)/shard_map/pallas_call | solution.py:241
  55.3 1.5 %collective-permute-start.7 = (bf16[512,256]{1,0:T(8,128)(2,1)S(1)}, bf16[512,256]{1,0:T(8,128)(2,1)S(1)}, u32[]{:S(2)}, u32[]{:S(2)}) collective-permute-start(bf16[512,256]{1,0:T(8,128)(2,1)S(1)} %get-tuple-element.30), channel_id=1, source_target_pairs={{0,2},{2,4},{4,6},{6,8},{8,10},{10,12},{12,14},{14,16},{16,18},{18... | collective-permute-start | bytes 786440 | tf_op jit(solution)/shard_map/ppermute | solution.py:22
  56.8 2.3 %collective-permute-done.5.refs_0_ = bf16[512,256]{1,0:T(8,128)(2,1)S(1)} collective-permute-done((bf16[512,256]{1,0:T(8,128)(2,1)S(1)}, bf16[512,256]{1,0:T(8,128)(2,1)S(1)}, u32[]{:S(2)}, u32[]{:S(2)}) %collective-permute-start.5) | collective-permute-done | bytes 262176 | tf_op jit(solution)/shard_map/ppermute | solution.py:33
  59.1 0.8 %shard_map.70 = (bf16[512,256]{1,0:T(8,128)(2,1)S(1)}, bf16[512,256]{1,0:T(8,128)(2,1)S(1)}) custom-call(s32[1]{0:T(128)} %bitcast.1.me, bf16[512,1024]{1,0:T(8,128)(2,1)S(1)} %shard_map.66.left, f32[512,1024]{1,0:T(8,128)S(1)} %shard_map.67.mine, bf16[256,512]{1,0:T(8,128)(2,1)S(1)} %bitcast.12, bf16[512,256]{1,0:T(8,128)(2,1)S(1)} %collective-permute-done.5.refs_0_, ...), custom_call_target="tpu_custom_call" | custom-call | flops 6291456 | bytes 73728 | tf_op jit(solution)/shard_map/pallas_call | solution.py:241
  59.9 1.2 %collective-permute-start.10 = (bf16[512,256]{1,0:T(8,128)(2,1)S(1)}, bf16[512,256]{1,0:T(8,128)(2,1)S(1)}, u32[]{:S(2)}, u32[]{:S(2)}) collective-permute-start(bf16[512,256]{1,0:T(8,128)(2,1)S(1)} %get-tuple-element.33), channel_id=1, source_target_pairs={{0,2},{2,4},{4,6},{6,8},{8,10},{10,12},{12,14},{14,16},{16,18},{18... | collective-permute-start | bytes 786440 | tf_op jit(solution)/shard_map/ppermute | solution.py:27
  61.1 0.8 %collective-permute-done.6.refs_3_ = bf16[512,512]{1,0:T(8,128)(2,1)S(1)} collective-permute-done((bf16[512,512]{1,0:T(8,128)(2,1)S(1)}, bf16[512,512]{1,0:T(8,128)(2,1)S(1)}, u32[]{:S(2)}, u32[]{:S(2)}) %collective-permute-start.6) | collective-permute-done | bytes 524320 | tf_op jit(solution)/shard_map/ppermute | solution.py:27
  61.9 0.6 shard_map.74
  62.5 2.1 %collective-permute-start.12 = (bf16[112,1024]{1,0:T(8,128)(2,1)S(1)}, bf16[112,1024]{1,0:T(8,128)(2,1)S(1)}, u32[]{:S(2)}, u32[]{:S(2)}) collective-permute-start(bf16[112,1024]{1,0:T(8,128)(2,1)S(1)} %shard_map.74), channel_id=1, source_target_pairs={{0,1},{1,0},{2,3},{3,2},{4,5},{5,4},{6,7},{7,6},{8,9},{9,8},{10,11... | collective-permute-start | bytes 688136 | tf_op jit(solution)/shard_map/ppermute | solution.py:40
  64.7 1.1 %shard_map.71 = (f32[512,1024]{1,0:T(8,128)S(1)}, bf16[1024,256]{1,0:T(8,128)(2,1)S(1)}) custom-call(s32[1]{0:T(128)} %bitcast.1.me, bf16[512,512]{1,0:T(8,128)(2,1)S(1)} %get-tuple-element.24.refs_0_, bf16[512,256]{1,0:T(8,128)(2,1)S(1)} %get-tuple-element.26.refs_1_, bf16[512,256]{1,0:T(8,128)(2,1)S(1)} %get-tuple-element.28.refs_2_, ...), custom_call_target="tpu_custom_call" | custom-call | flops 805306368 | bytes 102400 | tf_op jit(solution)/shard_map/pallas_call | solution.py:241
  65.7 3.0 %collective-permute-done.10.refs_0_ = bf16[512,256]{1,0:T(8,128)(2,1)S(1)} collective-permute-done((bf16[512,256]{1,0:T(8,128)(2,1)S(1)}, bf16[512,256]{1,0:T(8,128)(2,1)S(1)}, u32[]{:S(2)}, u32[]{:S(2)}) %collective-permute-start.10) | collective-permute-done | bytes 262176 | tf_op jit(solution)/shard_map/ppermute | solution.py:27
  69.3 2.2 %collective-permute-start.15 = (bf16[80,1024]{1,0:T(8,128)(2,1)S(1)}, bf16[80,1024]{1,0:T(8,128)(2,1)S(1)}, u32[]{:S(2)}, u32[]{:S(2)}) collective-permute-start(bf16[80,1024]{1,0:T(8,128)(2,1)S(1)} %get-tuple-element.38), channel_id=1, source_target_pairs={{0,1},{1,0},{2,3},{3,2},{4,5},{5,4},{6,7},{7,6},{8,9},{9,8},{10,11... | collective-permute-start | bytes 491528 | tf_op jit(solution)/shard_map/ppermute | solution.py:40
  71.5 1.9 %collective-permute-start.13 = (bf16[112,256]{1,0:T(8,128)(2,1)S(1)}, bf16[112,256]{1,0:T(8,128)(2,1)S(1)}, u32[]{:S(2)}, u32[]{:S(2)}) collective-permute-start(bf16[112,256]{1,0:T(8,128)(2,1)S(1)} %get-tuple-element.36), channel_id=1, source_target_pairs={{0,1},{1,0},{2,3},{3,2},{4,5},{5,4},{6,7},{7,6},{8,9},{9,8},{10,11... | collective-permute-start | bytes 172040 | tf_op jit(solution)/shard_map/ppermute | solution.py:40
  73.8 4.4 %collective-permute-done.11.refs_0_ = f32[8,128]{1,0:T(8,128)S(1)} collective-permute-done((f32[8,128]{1,0:T(8,128)S(1)}, f32[8,128]{1,0:T(8,128)S(1)}, u32[]{:S(2)}, u32[]{:S(2)}) %collective-permute-start.11) | collective-permute-done | bytes 4128 | tf_op jit(solution)/shard_map/ppermute | solution.py:40
  78.3 1.2 %shard_map.75 = f32[256,1024]{1,0:T(8,128)} custom-call(f32[256,1024]{1,0:T(8,128)S(1)} %shard_map.73.base, bf16[1024,256]{1,0:T(8,128)(2,1)S(1)} %get-tuple-element.32.right_rest, f32[8,128]{1,0:T(8,128)S(1)} %collective-permute-done.11.refs_0_, bf16[112,1024]{1,0:T(8,128)(2,1)S(1)} %collective-permute-done.12.refs_1_, ...), custom_call_target="tpu_custom_call" | custom-call | flops 1048576 | bytes 50112 | tf_op jit(solution)/shard_map/pallas_call | solution.py:241
  (28 shorter events, 1.4 us)
Async XLA Ops:
  0.0 27.2 %collective-permute-start.2 = (bf16[512,1024]{1,0:T(8,128)(2,1)}, bf16[512,1024]{1,0:T(8,128)(2,1)S(1)}, u32[]{:S(2)}, u32[]{:S(2)}) collective-permute-start(bf16[512,1024]{1,0:T(8,128)(2,1)} %bitcast.20), channel_id=1, source_target_pairs={{0,1},{1,0},{2,3},{3,2},{4,5},{5,4},{6,7},{7,6},{8,9},{9,8},{10,11... | collective-permute-start | bytes 3145736 | tf_op jit(solution)/shard_map/ppermute | solution.py:33
  3.0 37.5 %collective-permute-start = (bf16[512,1024]{1,0:T(8,128)(2,1)}, bf16[512,1024]{1,0:T(8,128)(2,1)S(1)}, u32[]{:S(2)}, u32[]{:S(2)}) collective-permute-start(bf16[512,1024]{1,0:T(8,128)(2,1)} %bitcast.18), channel_id=1, source_target_pairs={{2,0},{4,2},{6,4},{8,6},{10,8},{12,10},{14,12},{16,14},{18,16},{20... | collective-permute-start | bytes 3145736 | tf_op jit(solution)/shard_map/ppermute | solution.py:22
  4.3 1.0 %copy-start = (bf16[1,256,512]{2,1,0:T(8,128)(2,1)S(1)}, bf16[1,256,512]{2,1,0:T(8,128)(2,1)}, u32[]{:S(2)}) copy-start(bf16[1,256,512]{2,1,0:T(8,128)(2,1)} %param.9) | copy-start | bytes 786436
  5.2 1.2 %copy-start.2 = (bf16[1,512,1024]{2,1,0:T(8,128)(2,1)S(1)}, bf16[1,512,1024]{2,1,0:T(8,128)(2,1)}, u32[]{:S(2)}) copy-start(bf16[1,512,1024]{2,1,0:T(8,128)(2,1)} %param.8) | copy-start | bytes 3145732
  6.4 0.9 %copy-start.5 = (bf16[1,256,512]{2,1,0:T(8,128)(2,1)S(1)}, bf16[1,256,512]{2,1,0:T(8,128)(2,1)}, u32[]{:S(2)}) copy-start(bf16[1,256,512]{2,1,0:T(8,128)(2,1)} %param.7) | copy-start | bytes 786436
  7.4 34.4 %copy-start.6 = (bf16[1,1,512,1024]{3,2,1,0:T(8,128)(2,1)S(1)}, bf16[1,1,512,1024]{3,2,1,0:T(8,128)(2,1)}, u32[]{:S(2)}) copy-start(bf16[1,1,512,1024]{3,2,1,0:T(8,128)(2,1)} %param.6) | copy-start | bytes 3145732
  7.4 34.4 %copy-start.7 = (bf16[1,512,1024]{2,1,0:T(8,128)(2,1)S(1)}, bf16[1,512,1024]{2,1,0:T(8,128)(2,1)}, u32[]{:S(2)}) copy-start(bf16[1,512,1024]{2,1,0:T(8,128)(2,1)} %param.10) | copy-start | bytes 3145732
  7.6 30.8 %collective-permute-start.1 = (bf16[512,512]{1,0:T(8,128)(2,1)S(1)}, bf16[512,512]{1,0:T(8,128)(2,1)S(1)}, u32[]{:S(2)}, u32[]{:S(2)}) collective-permute-start(bf16[512,512]{1,0:T(8,128)(2,1)S(1)} %get-tuple-element.22), channel_id=1, source_target_pairs={{0,1},{1,0},{2,3},{3,2},{4,5},{5,4},{6,7},{7,6},{8,9},{9,8},{10,11... | collective-permute-start | bytes 1572872 | tf_op jit(solution)/shard_map/ppermute | solution.py:33
  7.7 41.9 %collective-permute-start.3 = (bf16[512,512]{1,0:T(8,128)(2,1)S(1)}, bf16[512,512]{1,0:T(8,128)(2,1)S(1)}, u32[]{:S(2)}, u32[]{:S(2)}) collective-permute-start(bf16[512,512]{1,0:T(8,128)(2,1)S(1)} %get-tuple-element.23), channel_id=1, source_target_pairs={{0,1},{1,0},{2,3},{3,2},{4,5},{5,4},{6,7},{7,6},{8,9},{9,8},{10,11... | collective-permute-start | bytes 1572872 | tf_op jit(solution)/shard_map/ppermute | solution.py:33
  9.7 51.3 %collective-permute-start.8 = (bf16[512,1024]{1,0:T(8,128)(2,1)}, bf16[512,1024]{1,0:T(8,128)(2,1)S(1)}, u32[]{:S(2)}, u32[]{:S(2)}) collective-permute-start(bf16[512,1024]{1,0:T(8,128)(2,1)} %bitcast.21), channel_id=1, source_target_pairs={{0,2},{2,4},{4,6},{6,8},{8,10},{10,12},{12,14},{14,16},{16,18},{18... | collective-permute-start | bytes 3145736 | tf_op jit(solution)/shard_map/ppermute | solution.py:22
  27.2 34.7 %collective-permute-start.9 = (bf16[512,1024]{1,0:T(8,128)(2,1)S(1)}, bf16[512,1024]{1,0:T(8,128)(2,1)S(1)}, u32[]{:S(2)}, u32[]{:S(2)}) collective-permute-start(bf16[512,1024]{1,0:T(8,128)(2,1)S(1)} %collective-permute-done.2.refs_1_), channel_id=1, source_target_pairs={{0,2},{2,4},{4,6},{6,8},{8,10},{10,12},{12,14},{14,16},{16,18},{18... | collective-permute-start | bytes 3145736 | tf_op jit(solution)/shard_map/ppermute | solution.py:22
  38.4 16.0 %collective-permute-start.4 = (bf16[512,256]{1,0:T(8,128)(2,1)S(1)}, bf16[512,256]{1,0:T(8,128)(2,1)S(1)}, u32[]{:S(2)}, u32[]{:S(2)}) collective-permute-start(bf16[512,256]{1,0:T(8,128)(2,1)S(1)} %get-tuple-element.25), channel_id=1, source_target_pairs={{0,1},{1,0},{2,3},{3,2},{4,5},{5,4},{6,7},{7,6},{8,9},{9,8},{10,11... | collective-permute-start | bytes 786440 | tf_op jit(solution)/shard_map/ppermute | solution.py:33
  41.8 3.6 %copy-start.3 = (bf16[1,512,1024]{2,1,0:T(8,128)(2,1)S(1)}, bf16[1,512,1024]{2,1,0:T(8,128)(2,1)}, u32[]{:S(2)}) copy-start(bf16[1,512,1024]{2,1,0:T(8,128)(2,1)} %param.8) | copy-start | bytes 3145732
  45.4 4.3 %copy-start.1 = (bf16[1,256,512]{2,1,0:T(8,128)(2,1)S(1)}, bf16[1,256,512]{2,1,0:T(8,128)(2,1)}, u32[]{:S(2)}) copy-start(bf16[1,256,512]{2,1,0:T(8,128)(2,1)} %param.9) | copy-start | bytes 786436
  50.5 11.4 %collective-permute-start.6 = (bf16[512,512]{1,0:T(8,128)(2,1)S(1)}, bf16[512,512]{1,0:T(8,128)(2,1)S(1)}, u32[]{:S(2)}, u32[]{:S(2)}) collective-permute-start(bf16[512,512]{1,0:T(8,128)(2,1)S(1)} %get-tuple-element.29), channel_id=1, source_target_pairs={{0,2},{2,4},{4,6},{6,8},{8,10},{10,12},{12,14},{14,16},{16,18},{18... | collective-permute-start | bytes 1572872 | tf_op jit(solution)/shard_map/ppermute | solution.py:27
  50.6 8.4 %collective-permute-start.5 = (bf16[512,256]{1,0:T(8,128)(2,1)S(1)}, bf16[512,256]{1,0:T(8,128)(2,1)S(1)}, u32[]{:S(2)}, u32[]{:S(2)}) collective-permute-start(bf16[512,256]{1,0:T(8,128)(2,1)S(1)} %get-tuple-element.27), channel_id=1, source_target_pairs={{0,1},{1,0},{2,3},{3,2},{4,5},{5,4},{6,7},{7,6},{8,9},{9,8},{10,11... | collective-permute-start | bytes 786440 | tf_op jit(solution)/shard_map/ppermute | solution.py:33
  55.3 5.8 %collective-permute-start.7 = (bf16[512,256]{1,0:T(8,128)(2,1)S(1)}, bf16[512,256]{1,0:T(8,128)(2,1)S(1)}, u32[]{:S(2)}, u32[]{:S(2)}) collective-permute-start(bf16[512,256]{1,0:T(8,128)(2,1)S(1)} %get-tuple-element.30), channel_id=1, source_target_pairs={{0,2},{2,4},{4,6},{6,8},{8,10},{10,12},{12,14},{14,16},{16,18},{18... | collective-permute-start | bytes 786440 | tf_op jit(solution)/shard_map/ppermute | solution.py:22
  59.9 8.8 %collective-permute-start.10 = (bf16[512,256]{1,0:T(8,128)(2,1)S(1)}, bf16[512,256]{1,0:T(8,128)(2,1)S(1)}, u32[]{:S(2)}, u32[]{:S(2)}) collective-permute-start(bf16[512,256]{1,0:T(8,128)(2,1)S(1)} %get-tuple-element.33), channel_id=1, source_target_pairs={{0,2},{2,4},{4,6},{6,8},{8,10},{10,12},{12,14},{14,16},{16,18},{18... | collective-permute-start | bytes 786440 | tf_op jit(solution)/shard_map/ppermute | solution.py:27
  62.5 15.7 %collective-permute-start.12 = (bf16[112,1024]{1,0:T(8,128)(2,1)S(1)}, bf16[112,1024]{1,0:T(8,128)(2,1)S(1)}, u32[]{:S(2)}, u32[]{:S(2)}) collective-permute-start(bf16[112,1024]{1,0:T(8,128)(2,1)S(1)} %shard_map.74), channel_id=1, source_target_pairs={{0,1},{1,0},{2,3},{3,2},{4,5},{5,4},{6,7},{7,6},{8,9},{9,8},{10,11... | collective-permute-start | bytes 688136 | tf_op jit(solution)/shard_map/ppermute | solution.py:40
  65.7 7.8 %copy-start.4 = (f32[1,256,1024]{2,1,0:T(8,128)S(1)}, f32[1,256,1024]{2,1,0:T(8,128)}, u32[]{:S(2)}) copy-start(f32[1,256,1024]{2,1,0:T(8,128)} %param.11) | copy-start | bytes 3145732
  69.3 8.9 %collective-permute-start.15 = (bf16[80,1024]{1,0:T(8,128)(2,1)S(1)}, bf16[80,1024]{1,0:T(8,128)(2,1)S(1)}, u32[]{:S(2)}, u32[]{:S(2)}) collective-permute-start(bf16[80,1024]{1,0:T(8,128)(2,1)S(1)} %get-tuple-element.38), channel_id=1, source_target_pairs={{0,1},{1,0},{2,3},{3,2},{4,5},{5,4},{6,7},{7,6},{8,9},{9,8},{10,11... | collective-permute-start | bytes 491528 | tf_op jit(solution)/shard_map/ppermute | solution.py:40
  71.4 6.8 %collective-permute-start.14 = (bf16[64,1024]{1,0:T(8,128)(2,1)S(1)}, bf16[64,1024]{1,0:T(8,128)(2,1)S(1)}, u32[]{:S(2)}, u32[]{:S(2)}) collective-permute-start(bf16[64,1024]{1,0:T(8,128)(2,1)S(1)} %get-tuple-element.37), channel_id=1, source_target_pairs={{0,1},{1,0},{2,3},{3,2},{4,5},{5,4},{6,7},{7,6},{8,9},{9,8},{10,11... | collective-permute-start | bytes 393224 | tf_op jit(solution)/shard_map/ppermute | solution.py:40
  71.5 6.7 %collective-permute-start.13 = (bf16[112,256]{1,0:T(8,128)(2,1)S(1)}, bf16[112,256]{1,0:T(8,128)(2,1)S(1)}, u32[]{:S(2)}, u32[]{:S(2)}) collective-permute-start(bf16[112,256]{1,0:T(8,128)(2,1)S(1)} %get-tuple-element.36), channel_id=1, source_target_pairs={{0,1},{1,0},{2,3},{3,2},{4,5},{5,4},{6,7},{7,6},{8,9},{9,8},{10,11... | collective-permute-start | bytes 172040 | tf_op jit(solution)/shard_map/ppermute | solution.py:40
  73.5 4.8 %collective-permute-start.11 = (f32[8,128]{1,0:T(8,128)S(1)}, f32[8,128]{1,0:T(8,128)S(1)}, u32[]{:S(2)}, u32[]{:S(2)}) collective-permute-start(f32[8,128]{1,0:T(8,128)S(1)} %get-tuple-element.34.squares), channel_id=1, source_target_pairs={{0,1},{1,0},{2,3},{3,2},{4,5},{5,4},{6,7},{7,6},{8,9},{9,8},{10,11... | collective-permute-start | bytes 12296 | tf_op jit(solution)/shard_map/ppermute | solution.py:40
